TPU v7x, 256 devices: a whole 4x4x8 slice. The times are simulated.
256 devices in a mesh: row: 16 (over x_hi, z), col: 16 (over y, x_lo, core).
Axes of the slice: x: 4 (x_hi: 2, x_lo: 2; x = x_hi * 2 + x_lo), y: 4, z: 8, core: 2. Of those that a mesh axis runs over, the one named last changes fastest.
Arguments:
- pair: bfloat16 [512, 512, 128], P('row', 'col'), may hold values from -6 to 6
- residue_mask: int32 [512], replicated, may hold values 0 or 1
- cotangent: bfloat16 [512, 512, 128], P('row', 'col'), may hold values from -6 to 6
- w_in: bfloat16 [128, 512], replicated, may hold values from -0.5 to 0.5
- w_out: bfloat16 [128, 128], replicated, may hold values from -0.5 to 0.5
- w_gout: bfloat16 [128, 128], replicated, may hold values from -0.5 to 0.5
- gain_in: float32 [128], replicated, may hold values from 0.25 to 1.75
- bias_in: float32 [128], replicated, may hold values from -3 to 3
- gain_out: float32 [128], replicated, may hold values from 0.25 to 1.75
- bias_out: float32 [128], replicated, may hold values from -3 to 3
Outputs:
- output: bfloat16 [512, 512, 128], P('row', 'col')
- grad_pair: bfloat16 [512, 512, 128], P('row', 'col')
All inputs are finite; a program needn't handle non-finite values.
Results may differ from a plain program's by a relative error of at most 0.017.
Values may be sent and summed in bfloat16 or wider, within the bound.
A program may use at most 128 MiB of HBM per device.

v0:
```python
import jax
import jax.numpy as jnp
from jax import lax
from jax.sharding import PartitionSpec as P

epsilon = 1e-05


def from_root(value, axis, source):
    kept = jnp.where(lax.axis_index(axis) == source, value, 0).astype(value.dtype)
    return lax.psum(kept, axis)


def normalize(values, gain_vec, offset):
    average = jnp.mean(values, axis=-1, keepdims=True)
    centred = values - average
    inverse = lax.rsqrt(jnp.mean(centred * centred, axis=-1, keepdims=True) + epsilon)
    scaled = centred * inverse
    return (scaled * gain_vec + offset, scaled, inverse)


def norm_back(grad_norm, gain_vec, scaled, inverse):
    grad_scaled = grad_norm * gain_vec
    first_mean = jnp.mean(grad_scaled, axis=-1, keepdims=True)
    second_mean = jnp.mean(grad_scaled * scaled, axis=-1, keepdims=True)
    return (grad_scaled - first_mean - scaled * second_mean) * inverse


def per_device(
    pair, residue_mask, cotangent, w_in, w_out, w_gout, gain_in, bias_in, gain_out, bias_out
):
    hidden = w_out.shape[0]
    row_tile = pair.shape[0]
    col_tile = pair.shape[1]
    ratio = lax.axis_size("row") // lax.axis_size("col")
    row_index = lax.axis_index("row")
    col_index = lax.axis_index("col")
    valid = residue_mask.astype(jnp.float32)
    row_valid = lax.dynamic_slice_in_dim(valid, row_index * row_tile, row_tile)
    col_valid = lax.dynamic_slice_in_dim(valid, col_index * col_tile, col_tile)
    pair_mask = (row_valid[:, None] * col_valid[None, :])[..., None]
    normed, scaled_in, inverse_in = normalize(pair.astype(jnp.float32), gain_in, bias_in)
    normed = normed.astype(jnp.bfloat16)
    mixed = jnp.dot(normed, w_in, preferred_element_type=jnp.float32)
    projected = mixed[..., : 2 * hidden]
    gates = jax.nn.sigmoid(mixed[..., 2 * hidden :])
    branch = (gates * projected * pair_mask).astype(jnp.bfloat16)
    left = branch[..., :hidden]
    right = branch[..., hidden:]
    left_panel, right_rows = (
        lax.all_gather(left, "col", axis=1, tiled=True),
        lax.all_gather(right, "col", axis=1, tiled=True),
    )
    received = from_root(right_rows, "row", col_index * ratio + 0)
    tri = jnp.einsum("ikc,jkc->ijc", left_panel, received, preferred_element_type=jnp.float32)
    out_norm, scaled_out, inverse_out = normalize(tri, gain_out, bias_out)
    out_norm = out_norm.astype(jnp.bfloat16)
    outer_gate = jax.nn.sigmoid(jnp.dot(normed, w_gout, preferred_element_type=jnp.float32))
    outer_proj = jnp.dot(out_norm, w_out, preferred_element_type=jnp.float32)
    output = (outer_gate * outer_proj).astype(jnp.bfloat16)
    upstream = cotangent.astype(jnp.float32)
    grad_proj = (upstream * outer_gate).astype(jnp.bfloat16)
    grad_gate = (upstream * outer_proj * outer_gate * (1.0 - outer_gate)).astype(jnp.bfloat16)
    grad_outnorm = jnp.dot(grad_proj, w_out.T, preferred_element_type=jnp.float32)
    grad_tri = norm_back(grad_outnorm, gain_out, scaled_out, inverse_out).astype(jnp.bfloat16)
    grad_left = jnp.transpose(
        lax.psum_scatter(
            jnp.einsum(
                "ijc,jkc->kic", grad_tri, received, preferred_element_type=jnp.float32
            ).astype(jnp.bfloat16),
            "col",
            scatter_dimension=0,
            tiled=True,
        ).astype(jnp.float32),
        (1, 0, 2),
    )
    partial_right = jnp.einsum(
        "ijc,ikc->jkc", grad_tri, left_panel, preferred_element_type=jnp.float32
    )
    moved = lax.all_to_all(
        partial_right.astype(jnp.bfloat16), "col", split_axis=1, concat_axis=0, tiled=True
    ).astype(partial_right.dtype)
    grad_right = lax.psum_scatter(
        moved.astype(jnp.bfloat16), "row", scatter_dimension=0, tiled=True
    ).astype(jnp.float32)
    grad_branch = jnp.concatenate([grad_left, grad_right], axis=-1) * pair_mask
    grad_mixed = jnp.concatenate(
        [grad_branch * gates, grad_branch * projected * gates * (1.0 - gates)], axis=-1
    ).astype(jnp.bfloat16)
    grad_normed = jnp.dot(grad_mixed, w_in.T, preferred_element_type=jnp.float32) + jnp.dot(
        grad_gate, w_gout.T, preferred_element_type=jnp.float32
    )
    grad_pair = norm_back(grad_normed, gain_in, scaled_in, inverse_in).astype(jnp.bfloat16)
    return (output, grad_pair)


def solution(mesh):
    return jax.shard_map(
        per_device,
        mesh=mesh,
        in_specs=(
            P("row", "col", None),
            P(),
            P("row", "col", None),
            P(),
            P(),
            P(),
            P(),
            P(),
            P(),
            P(),
        ),
        out_specs=(P("row", "col", None), P("row", "col", None)),
        check_vma=False,
    )
```

profile of v0, /device:TPU:1, one launch (start us, length us, event | category | flops | bytes accessed | tf_op | source)
XLA Modules:
  0.0 634.0 jit_solution(18372231212449267089)
XLA Ops:
  7.2 0.7 convert_element_type.54
  7.9 1.2 convert_reduce_fusion
  9.1 1.3 fusion.21
  10.6 1.5 fusion.37
  12.4 0.9 fusion.49
  13.4 0.7 all-gather.5.cloned.1.call-update
  14.1 43.5 %all-gather.3.cloned.1.call-done = bf16[32,512,128]{2,1,0:T(8,128)(2,1)} async-done(((bf16[32,32,128]{2,1,0:T(8,128)(2,1)}), bf16[32,512,128]{2,1,0:T(8,128)(2,1)}) %all-gather.3.cloned.1.call-update) | async-done | bytes 4194320 | tf_op jit(solution)/shard_map/all_gather | solution.py:52
  57.6 2.2 broadcast_select_fusion
  59.9 40.1 %all-gather.5.cloned.1.call-done = bf16[32,512,128]{2,1,0:T(8,128)(2,1)} async-done(((bf16[32,32,128]{2,1,0:T(8,128)(2,1)}), bf16[32,512,128]{2,1,0:T(8,128)(2,1)}) %all-gather.5.cloned.1.call-update) | async-done | bytes 4194320 | tf_op jit(solution)/shard_map/all_gather | solution.py:51
  100.0 8.0 %copy.74 = bf16[32,512,128]{1,0,2:T(8,128)(2,1)} copy(bf16[32,512,128]{2,1,0:T(8,128)(2,1)} %all-gather.5.cloned.1.call-done) | data formatting | bytes 8388608 | tf_op jit(solution)/shard_map/all_gather | solution.py:51
  108.0 159.4 %all-reduce.2.cloned.1.call-done = bf16[32,512,128]{2,1,0:T(8,128)(2,1)} async-done(((bf16[32,512,128]{2,1,0:T(8,128)(2,1)}), bf16[32,512,128]{2,1,0:T(8,128)(2,1)}) %all-reduce.2.cloned.1.call-update) | async-done | bytes 4194320 | tf_op jit(solution)/shard_map/psum | solution.py:11
  267.4 7.9 %copy.73 = bf16[32,512,128]{1,0,2:T(8,128)(2,1)} copy(bf16[32,512,128]{2,1,0:T(8,128)(2,1)} %all-reduce.2.cloned.1.call-done) | data formatting | bytes 8388608 | tf_op jit(solution)/shard_map/psum | solution.py:11
  275.3 6.1 bitcast_reduce_fusion
  281.5 2.8 copy.75
  284.7 1.2 fusion.27
  286.0 2.2 multiply_convert_fusion.4
  288.2 0.8 copy-done.4
  289.0 1.6 fusion.48
  290.7 1.3 multiply_convert_fusion.3
  292.0 2.7 copy.88
  294.7 5.4 fusion.51
  300.1 7.9 %copy.86 = bf16[128,512,32]{0,1,2:T(8,128)(2,1)} copy(bf16[128,512,32]{1,2,0:T(8,128)(2,1)} %fusion.51) | data formatting | bytes 8388608 | tf_op jit(solution)/shard_map/ijc,jkc->kic/dot_general | solution.py:68
  308.3 5.4 convert_bitcast_fusion
  313.6 9.1 %copy.89 = bf16[32,512,128]{2,0,1:T(8,128)(2,1)} copy(bf16[32,512,128]{1,0,2:T(8,128)(2,1)} %convert_bitcast_fusion) | data formatting | bytes 8388608 | tf_op jit(solution)/shard_map/convert_element_type | solution.py:81
  322.7 94.5 %all_to_all.18 = bf16[32,512,128]{2,0,1:T(8,128)(2,1)S(1)} all-to-all(bf16[32,512,128]{2,0,1:T(8,128)(2,1)} %copy.89), channel_id=1, replica_groups=mesh['row'=16,'col'=16] {'col'}, dimensions={1} | all-to-all | bytes 8388608 | tf_op jit(solution)/shard_map/all_to_all | solution.py:80
  417.2 3.7 copy.91
  420.9 1.0 copy-done.3
  422.1 2.0 fusion.28
  424.1 198.7 %reduce-scatter.5.cloned.1.call-done = bf16[32,32,128]{2,1,0:T(8,128)(2,1)} async-done(((bf16[512,32,128]{2,1,0:T(8,128)(2,1)}), bf16[32,32,128]{2,1,0:T(8,128)(2,1)}) %reduce-scatter.5.cloned.1.call-update) | async-done | bytes 262160 | tf_op jit(solution)/shard_map/reduce_scatter | solution.py:83
  622.8 1.5 multiply_convert_fusion.1
  624.3 1.8 fusion.47
  626.2 1.3 fusion.20
  (42 shorter events, 1.6 us)
Async XLA Ops:
  7.2 3.5 copy-start
  7.2 50.4 %all-gather.3.cloned.1.call-start = ((), (), s32[]{:S(2)}) async-start(), calls=%async_computation.3 | async-start | bytes 4456448 | tf_op jit(solution)/shard_map/all_gather | solution.py:52
  9.1 50.8 %copy-start.6 = (f32[32,32]{1,0:T(8,128)}, f32[32,32]{1,0:T(8,128)S(1)}, u32[]{:S(2)}) copy-start(f32[32,32]{1,0:T(8,128)S(1)} %broadcast_multiply_fusion.6) | copy-start | bytes 12292
  10.4 49.4 %copy-start.8 = (f32[32,32]{1,0:T(8,128)}, f32[32,32]{1,0:T(8,128)S(1)}, u32[]{:S(2)}) copy-start(f32[32,32]{1,0:T(8,128)S(1)} %add_rsqrt_fusion.1) | copy-start | bytes 12292
  10.6 2.7 copy-start.10
  13.3 86.7 %all-gather.5.cloned.1.call-start = ((), (), s32[]{:S(2)}) async-start(), calls=%async_computation.5 | async-start | bytes 4456448 | tf_op jit(solution)/shard_map/all_gather | solution.py:51
  14.1 253.3 %all-reduce.2.cloned.1.call-start = ((), (), s32[]{:S(2)}) async-start(), calls=%async_computation.4 | async-start | bytes 8388608 | tf_op jit(solution)/shard_map/psum | solution.py:11
  59.9 364.2 %reduce-scatter.3.cloned.1.call-start = ((), (), s32[]{:S(2)}) async-start(), calls=%async_computation.6 | async-start | bytes 4456448 | tf_op jit(solution)/shard_map/reduce_scatter | solution.py:67
  281.4 4.6 copy-start.1
  286.0 4.7 copy-start.2
  288.2 0.8 copy-start.4
  308.0 314.8 %reduce-scatter.5.cloned.1.call-start = ((), (), s32[]{:S(2)}) async-start(), calls=%async_computation.7 | async-start | bytes 4456448 | tf_op jit(solution)/shard_map/reduce_scatter | solution.py:83
  420.9 1.0 copy-start.3
  420.9 1.2 copy-start.5
  420.9 203.5 %copy-start.7 = (f32[32,32]{1,0:T(8,128)S(1)}, f32[32,32]{1,0:T(8,128)}, u32[]{:S(2)}) copy-start(f32[32,32]{1,0:T(8,128)} %copy-done.6) | copy-start | bytes 12292
  424.1 202.0 %copy-start.9 = (f32[32,32]{1,0:T(8,128)S(1)}, f32[32,32]{1,0:T(8,128)}, u32[]{:S(2)}) copy-start(f32[32,32]{1,0:T(8,128)} %copy-done.8) | copy-start | bytes 12292
Sparse Core Ops, SparseCore 0:
  13.4 44.1 all-gather.2
  60.0 39.9 all-gather.4
  102.7 164.6 all-reduce.1
  308.1 95.2 reduce-scatter.2
  421.0 201.7 reduce-scatter.4
where the time goes:
time: 639 us; the launch traced here: 634 us
  waiting for transfers between devices  442 us (69%)
  blocking collectives  94.5 us (15%)
  local copies, waits for them, and re-layouts  45.2 us (7%)
  matrix products  27.2 us (4%)
  between operations  14 us (2%)
  other arithmetic  10.3 us (2%)
    reduce_scatter x1, waiting for transfers between devices, per_device(): lax.psum_scatter(moved.astype(jnp.bfloat16), 'row', scatter_dimension=0,...  199 us
    psum x1, waiting for transfers between devices, from_root(): return lax.psum(kept, axis)  159 us
    all_to_all x1, blocking collectives, per_device(): lax.all_to_all(partial_right.astype(jnp.bfloat16), 'col', split_axis=1, c...  94.5 us
    all_gather x1, waiting for transfers between devices, per_device(): lax.all_gather(right, 'col', axis=1, tiled=True)  43.5 us
    all_gather x1, waiting for transfers between devices, per_device(): lax.all_gather(left, 'col', axis=1, tiled=True)  40.1 us
  transfers between devices with their start and end apart: 5, of which 4 were waited for; matrix products, arithmetic and copies ran while one was open for 5% of the time, Pallas kernels for 0%

commit v1 on v0

--- a/solution.py
+++ b/solution.py
@@ -4,11 +4,6 @@
 from jax.sharding import PartitionSpec as P
 
 epsilon = 1e-05
-
-
-def from_root(value, axis, source):
-    kept = jnp.where(lax.axis_index(axis) == source, value, 0).astype(value.dtype)
-    return lax.psum(kept, axis)
 
 
 def normalize(values, gain_vec, offset):
@@ -26,13 +21,38 @@
     return (grad_scaled - first_mean - scaled * second_mean) * inverse
 
 
+def to_channels(tile):
+    t, rows, cols, chans = tile.shape
+    wide = lax.all_to_all(tile, "col", split_axis=3, concat_axis=2, tiled=True)
+    own = wide.shape[3]
+    parts = lax.axis_size("row")
+    halves = parts // own
+    split = wide.reshape(t, rows, halves, wide.shape[2] // halves, own)
+    split = jnp.transpose(split, (4, 2, 0, 1, 3)).reshape(parts, t, rows, -1)
+    moved = lax.all_to_all(split, "row", split_axis=0, concat_axis=0, tiled=True)
+    return jnp.transpose(moved, (1, 0, 2, 3)).reshape(t, parts * rows, -1)
+
+
+def from_channels(whole, own):
+    parts = lax.axis_size("row")
+    halves = parts // own
+    t, all_rows, wide = whole.shape
+    rows = all_rows // parts
+    split = jnp.transpose(whole.reshape(t, parts, rows, wide), (1, 0, 2, 3))
+    moved = lax.all_to_all(split, "row", split_axis=0, concat_axis=0, tiled=True)
+    moved = moved.reshape(own, halves, t, rows, wide)
+    moved = jnp.transpose(moved, (2, 3, 1, 4, 0)).reshape(t, rows, halves * wide, own)
+    return lax.all_to_all(moved, "col", split_axis=2, concat_axis=3, tiled=True)
+
+
 def per_device(
     pair, residue_mask, cotangent, w_in, w_out, w_gout, gain_in, bias_in, gain_out, bias_out
 ):
     hidden = w_out.shape[0]
     row_tile = pair.shape[0]
     col_tile = pair.shape[1]
-    ratio = lax.axis_size("row") // lax.axis_size("col")
+    rows = lax.axis_size("row")
+    own = hidden // lax.axis_size("col")
     row_index = lax.axis_index("row")
     col_index = lax.axis_index("col")
     valid = residue_mask.astype(jnp.float32)
@@ -45,14 +65,16 @@
     projected = mixed[..., : 2 * hidden]
     gates = jax.nn.sigmoid(mixed[..., 2 * hidden :])
     branch = (gates * projected * pair_mask).astype(jnp.bfloat16)
-    left = branch[..., :hidden]
-    right = branch[..., hidden:]
-    left_panel, right_rows = (
-        lax.all_gather(left, "col", axis=1, tiled=True),
-        lax.all_gather(right, "col", axis=1, tiled=True),
-    )
-    received = from_root(right_rows, "row", col_index * ratio + 0)
-    tri = jnp.einsum("ikc,jkc->ijc", left_panel, received, preferred_element_type=jnp.float32)
+    both = to_channels(jnp.stack([branch[..., :hidden], branch[..., hidden:]]))
+    left, right = both[0], both[1]
+    half = row_index % 2
+    swap = [(r, r ^ 1) for r in range(rows)]
+    tri_all = jnp.einsum("ik,jk->ij", left, right, preferred_element_type=jnp.float32)
+    width = tri_all.shape[1] // 2
+    mine = lax.dynamic_slice_in_dim(tri_all, half * width, width, axis=1)
+    theirs = lax.dynamic_slice_in_dim(tri_all, (1 - half) * width, width, axis=1)
+    tri_half = mine + lax.ppermute(theirs, "row", swap)
+    tri = from_channels(tri_half.astype(jnp.bfloat16)[None], own)[0].astype(jnp.float32)
     out_norm, scaled_out, inverse_out = normalize(tri, gain_out, bias_out)
     out_norm = out_norm.astype(jnp.bfloat16)
     outer_gate = jax.nn.sigmoid(jnp.dot(normed, w_gout, preferred_element_type=jnp.float32))
@@ -63,27 +85,16 @@
     grad_gate = (upstream * outer_proj * outer_gate * (1.0 - outer_gate)).astype(jnp.bfloat16)
     grad_outnorm = jnp.dot(grad_proj, w_out.T, preferred_element_type=jnp.float32)
     grad_tri = norm_back(grad_outnorm, gain_out, scaled_out, inverse_out).astype(jnp.bfloat16)
-    grad_left = jnp.transpose(
-        lax.psum_scatter(
-            jnp.einsum(
-                "ijc,jkc->kic", grad_tri, received, preferred_element_type=jnp.float32
-            ).astype(jnp.bfloat16),
-            "col",
-            scatter_dimension=0,
-            tiled=True,
-        ).astype(jnp.float32),
-        (1, 0, 2),
-    )
-    partial_right = jnp.einsum(
-        "ijc,ikc->jkc", grad_tri, left_panel, preferred_element_type=jnp.float32
-    )
-    moved = lax.all_to_all(
-        partial_right.astype(jnp.bfloat16), "col", split_axis=1, concat_axis=0, tiled=True
-    ).astype(partial_right.dtype)
-    grad_right = lax.psum_scatter(
-        moved.astype(jnp.bfloat16), "row", scatter_dimension=0, tiled=True
-    ).astype(jnp.float32)
-    grad_branch = jnp.concatenate([grad_left, grad_right], axis=-1) * pair_mask
+    grad_half = to_channels(grad_tri[None])[0]
+    other = lax.ppermute(grad_half, "row", swap)
+    first = jnp.where(half == 0, grad_half, other)
+    second = jnp.where(half == 0, other, grad_half)
+    grad_all = jnp.concatenate([first, second], axis=1)
+    grad_left = jnp.einsum("ij,jk->ik", grad_all, right, preferred_element_type=jnp.float32)
+    grad_right = jnp.einsum("ij,ik->jk", grad_all, left, preferred_element_type=jnp.float32)
+    grads = from_channels(jnp.stack([grad_left, grad_right]).astype(jnp.bfloat16), own)
+    grads = grads.astype(jnp.float32)
+    grad_branch = jnp.concatenate([grads[0], grads[1]], axis=-1) * pair_mask
     grad_mixed = jnp.concatenate(
         [grad_branch * gates, grad_branch * projected * gates * (1.0 - gates)], axis=-1
     ).astype(jnp.bfloat16)

time: 639 us -> 217 us (0.34)
  waiting for transfers between devices: 442 us -> 34.6 us
  starting transfers between devices: 0.38 us -> 21.7 us
  matrix products: 27.2 us -> 7.69 us
  between operations: 14 us -> 1.24 us
    reduce_scatter x2 -> x0, waiting for transfers between devices: 199 us -> none  [the longest x1 199 us: per_device(): lax.psum_scatter(moved.astype(jnp.bfloat16), 'row', scatter_dimension=0,...]
    psum x1 -> x0, waiting for transfers between devices: 159 us -> none  [from_root(): return lax.psum(kept, axis)]
    all_gather x2 -> x0, waiting for transfers between devices: 83.6 us -> none  [the longest x1 43.5 us: per_device(): lax.all_gather(right, 'col', axis=1, tiled=True)]
    all_to_all x0 -> x2, waiting for transfers between devices: none -> 21.8 us  [the longest x1 14.2 us: to_channels(): lax.all_to_all(split, 'row', split_axis=0, concat_axis=0, tiled=True)]
    all_to_all x0 -> x2, starting transfers between devices: none -> 17.6 us  [the longest x1 10.5 us: to_channels(): lax.all_to_all(split, 'row', split_axis=0, concat_axis=0, tiled=True)]
    dot_general x3, matrix products: 16.9 us -> 0.92 us  [the longest x1 0.33 us: per_device(): jnp.einsum('ik,jk->ij', left, right, preferred_element_type=jnp.float32)]
    ppermute x0 -> x2, waiting for transfers between devices: none -> 12.8 us  [the longest x1 9.09 us: per_device(): tri_half = mine + lax.ppermute(theirs, 'row', swap)]
    dot_general x2 -> x1, local copies, waits for them, and re-layouts: 10.7 us -> 0.21 us  [per_device(): jnp.einsum('ij,ik->jk', grad_all, left, preferred_element_type=jnp.float32)]
  transfers between devices with their start and end apart: 5 -> 4, of which waited for: 4 -> 4; matrix products, arithmetic and copies ran while one was open for 5% -> 1% of each run, Pallas kernels for 0% -> 0%
where the time goes in v1:
time: 217 us
  blocking collectives  93.4 us (43%)
  local copies, waits for them, and re-layouts  50.6 us (23%)
  waiting for transfers between devices  34.6 us (16%)
  starting transfers between devices  21.7 us (10%)
  matrix products  7.69 us (4%)
  other arithmetic  7.44 us (3%)
    all_to_all x2, blocking collectives, from_channels(): lax.all_to_all(split, 'row', split_axis=0, concat_axis=0, tiled=True)  36.5 us
    all_to_all x2, blocking collectives, to_channels(): wide = lax.all_to_all(tile, 'col', split_axis=3, concat_axis=2, tiled=True)  27.1 us
    all_to_all x1, blocking collectives, from_channels(): return lax.all_to_all(moved, 'col', split_axis=2, concat_axis=3, tiled=True)  15.9 us
    all_to_all x1, waiting for transfers between devices, to_channels(): lax.all_to_all(split, 'row', split_axis=0, concat_axis=0, tiled=True)  14.2 us
    all_to_all x1, blocking collectives, to_channels(): lax.all_to_all(split, 'row', split_axis=0, concat_axis=0, tiled=True)  13.9 us
    unnamed x54, local copies, waits for them, and re-layouts  11.6 us
    all_to_all x1, starting transfers between devices, to_channels(): lax.all_to_all(split, 'row', split_axis=0, concat_axis=0, tiled=True)  10.5 us
    ppermute x1, waiting for transfers between devices, per_device(): tri_half = mine + lax.ppermute(theirs, 'row', swap)  9.09 us
  transfers between devices with their start and end apart: 4, of which 4 were waited for; matrix products, arithmetic and copies ran while one was open for 1% of the time, Pallas kernels for 0%

profile of v1, /device:TPU:1, one launch (start us, length us, event | category | flops | bytes accessed | tf_op | source)
XLA Modules:
  0.0 216.7 jit_solution(16916234812938632740)
XLA Ops:
  2.6 1.3 fusion.23
  4.1 1.5 fusion.39
  5.6 1.3 copy-done.1
  7.4 3.0 %copy.110 = bf16[2,32,32,128]{2,1,0,3:T(8,128)(2,1)S(1)} copy(bf16[2,32,32,128]{3,2,1,0:T(8,128)(2,1)S(1)} %pad_maximum_fusion) | data formatting | bytes 1048576 | tf_op jit(solution)/shard_map/stack | solution.py:68
  10.4 2.0 reshape.158
  12.3 16.5 %all_to_all.68 = bf16[16,2,8192]{2,1,0:T(2,128)(2,1)S(1)} all-to-all(bf16[16,2,8192]{2,1,0:T(2,128)(2,1)S(1)} %reshape.158), channel_id=1, replica_groups=mesh['row'=16,'col'=16] {'col'}, dimensions={0} | all-to-all | bytes 1048576 | tf_op jit(solution)/shard_map/all_to_all | solution.py:26
  29.9 2.7 %copy.112 = bf16[2,32,16,32,8]{3,2,4,1,0:T(8,128)(2,1)} copy(bf16[2,32,16,32,8]{3,1,0,4,2:T(8,128)(2,1)S(1)} %bitcast.118) | data formatting | bytes 1048576 | tf_op jit(solution)/shard_map/all_to_all | solution.py:26
  32.6 3.5 %reshape.139 = bf16[2,32,2,256,8]{3,2,4,1,0:T(2,128)(2,1)S(1)} reshape(bf16[2,32,16,32,8]{3,2,4,1,0:T(8,128)(2,1)} %copy.112) | data formatting | bytes 1048576 | tf_op jit(solution)/shard_map/reshape | solution.py:30
  37.0 10.5 %all-to-all-start.1 = ((bf16[16,2,32,256]{3,2,1,0:T(8,128)(2,1)}), bf16[16,2,32,256]{3,2,1,0:T(8,128)(2,1)S(1)}, u32[]{:S(2)}, u32[]{:S(2)}) async-start(bf16[16,2,32,256]{3,2,1,0:T(8,128)(2,1)} %bitcast.8), calls=%async_computation.1 | async-start | bytes 1048576 | tf_op jit(solution)/shard_map/all_to_all | solution.py:32
  47.5 14.2 %all-to-all-done.1 = bf16[16,2,32,256]{3,2,1,0:T(8,128)(2,1)S(1)} async-done(((bf16[16,2,32,256]{3,2,1,0:T(8,128)(2,1)}), bf16[16,2,32,256]{3,2,1,0:T(8,128)(2,1)S(1)}, u32[]{:S(2)}, u32[]{:S(2)}) %all-to-all-start.1) | async-done | bytes 524320 | tf_op jit(solution)/shard_map/all_to_all | solution.py:32
  62.1 2.1 collective-permute-start
  64.1 9.1 %collective-permute-done = f32[512,256]{1,0:T(8,128)S(1)} collective-permute-done((f32[512,256]{1,0:T(8,128)S(1)}, f32[512,256]{1,0:T(8,128)S(1)}, u32[]{:S(2)}, u32[]{:S(2)}) %collective-permute-start) | collective-permute-done | bytes 524320 | tf_op jit(solution)/shard_map/ppermute | solution.py:76
  73.3 15.8 %all_to_all.69 = bf16[16,1,32,256]{3,2,1,0:T(8,128)(2,1)S(1)} all-to-all(bf16[16,1,32,256]{3,2,1,0:T(8,128)(2,1)S(1)} %bitcast.137), channel_id=1, replica_groups=mesh['row'=16,'col'=16] {'row'}, dimensions={0} | all-to-all | bytes 524288 | tf_op jit(solution)/shard_map/all_to_all | solution.py:42
  91.2 15.9 %all_to_all.70 = bf16[16,2,4096]{2,1,0:T(2,128)(2,1)S(1)} all-to-all(bf16[16,2,4096]{2,1,0:T(2,128)(2,1)S(1)} %reshape.160), channel_id=1, replica_groups=mesh['row'=16,'col'=16] {'col'}, dimensions={0} | all-to-all | bytes 524288 | tf_op jit(solution)/shard_map/all_to_all | solution.py:45
  110.2 2.2 %copy.142 = f32[1,32,32,16,8]{2,4,3,1,0:T(8,128)} copy(f32[1,32,32,16,8]{2,3,4,1,0:T(8,128)S(1)} %bitcast.113) | data formatting | bytes 1048576 | tf_op jit(solution)/shard_map/convert_element_type | solution.py:77
  112.5 2.3 %copy.119 = f32[32,32,128]{2,1,0:T(8,128)S(1)} copy(f32[32,32,128]{1,2,0:T(8,128)} %bitcast.119) | data formatting | bytes 1048576 | tf_op jit(solution)/shard_map/convert_element_type | solution.py:77
  118.0 1.4 copy.120
  120.4 10.6 %all_to_all.71 = bf16[16,2,4096]{2,1,0:T(2,128)(2,1)S(1)} all-to-all(bf16[16,2,4096]{2,1,0:T(2,128)(2,1)S(1)} %reshape.162), channel_id=1, replica_groups=mesh['row'=16,'col'=16] {'col'}, dimensions={0} | all-to-all | bytes 524288 | tf_op jit(solution)/shard_map/all_to_all | solution.py:26
  133.0 13.9 %all_to_all.72 = bf16[16,1,32,256]{3,2,1,0:T(8,128)(2,1)S(1)} all-to-all(bf16[16,1,32,256]{3,2,1,0:T(8,128)(2,1)S(1)} %bitcast.141), channel_id=1, replica_groups=mesh['row'=16,'col'=16] {'row'}, dimensions={0} | all-to-all | bytes 524288 | tf_op jit(solution)/shard_map/all_to_all | solution.py:32
  146.8 2.1 collective-permute-start.1
  148.9 3.8 %collective-permute-done.1 = bf16[512,256]{1,0:T(8,128)(2,1)S(1)} collective-permute-done((bf16[512,256]{1,0:T(8,128)(2,1)S(1)}, bf16[512,256]{1,0:T(8,128)(2,1)S(1)}, u32[]{:S(2)}, u32[]{:S(2)}) %collective-permute-start.1) | collective-permute-done | bytes 262176 | tf_op jit(solution)/shard_map/ppermute | solution.py:89
  153.7 20.6 %all_to_all.73 = bf16[16,2,32,256]{3,2,1,0:T(8,128)(2,1)S(1)} all-to-all(bf16[16,2,32,256]{3,2,1,0:T(8,128)(2,1)S(1)} %copy.125), channel_id=1, replica_groups=mesh['row'=16,'col'=16] {'row'}, dimensions={0} | all-to-all | bytes 1048576 | tf_op jit(solution)/shard_map/all_to_all | solution.py:42
  174.6 2.2 copy.127
  176.8 2.7 %reshape.164 = bf16[16,2,8192]{2,1,0:T(2,128)(2,1)} reshape(bf16[512,2,8,32]{3,2,1,0:T(8,128)(2,1)S(1)} %bitcast.116) | data formatting | bytes 1048576
  179.5 7.1 %all-to-all-start.7 = ((bf16[16,2,8192]{2,1,0:T(2,128)(2,1)}), bf16[16,2,8192]{2,1,0:T(2,128)(2,1)S(1)}, u32[]{:S(2)}, u32[]{:S(2)}) async-start(bf16[16,2,8192]{2,1,0:T(2,128)(2,1)} %reshape.164), calls=%async_computation.7 | async-start | bytes 1048576 | tf_op jit(solution)/shard_map/all_to_all | solution.py:45
  186.6 2.2 %fusion.30 = f32[32,32,128]{2,1,0:T(8,128)} fusion(f32[32,32,128]{2,1,0:T(8,128)} %copy-done.4, f32[32,32,128]{2,1,0:T(8,128)S(1)} %fusion.28, bf16[32,32,128]{2,1,0:T(8,128)(2,1)} %param.12, bf16[128,128]{1,0:T(8,128)(2,1)} %param.15), kind=kOutput, calls=%fused_computation.58 | convolution fusion | flops 34340864 | bytes 1867776 | tf_op jit(solution)/shard_map/dot_general | solution.py:101
  188.8 7.6 %all-to-all-done.7 = bf16[16,2,8192]{2,1,0:T(2,128)(2,1)S(1)} async-done(((bf16[16,2,8192]{2,1,0:T(2,128)(2,1)}), bf16[16,2,8192]{2,1,0:T(2,128)(2,1)S(1)}, u32[]{:S(2)}, u32[]{:S(2)}) %all-to-all-start.7) | async-done | bytes 524320 | tf_op jit(solution)/shard_map/all_to_all | solution.py:45
  197.4 2.2 %copy.128 = bf16[2,32,512,8]{2,3,1,0:T(8,128)(2,1)S(1)} copy(bf16[2,32,512,8]{1,3,0,2:T(8,128)(2,1)S(1)} %bitcast.117) | data formatting | bytes 1048576 | tf_op jit(solution)/shard_map/all_to_all | solution.py:45
  199.6 2.5 %reshape.150 = f32[2,32,16,32,8]{3,2,4,1,0:T(8,128)} reshape(bf16[2,32,512,8]{2,3,1,0:T(8,128)(2,1)S(1)} %copy.128) | data formatting | bytes 1572864 | tf_op jit(solution)/shard_map/convert_element_type | solution.py:96
  202.1 4.0 %fusion.52 = (f32[1,32,32,16,8]{2,3,4,1,0:T(8,128)S(1)}, f32[1,32,32,16,8]{2,3,4,1,0:T(8,128)}) fusion(f32[2,32,32,16,8]{2,3,4,1,0:T(8,128)} %bitcast.114), kind=kLoop, calls=%fused_computation.91 | loop fusion | bytes 2097152 | tf_op jit(solution)/shard_map/slice | solution.py:97
  207.5 3.8 %copy.140 = f32[1,32,32,16,8]{2,4,3,1,0:T(8,128)} copy(f32[1,32,32,16,8]{2,3,4,1,0:T(8,128)} %get-tuple-element.7) | data formatting | bytes 1048576 | tf_op jit(solution)/shard_map/slice | solution.py:97
  211.3 2.3 %copy.132 = f32[32,32,128]{2,1,0:T(8,128)S(1)} copy(f32[32,32,128]{1,2,0:T(8,128)} %bitcast.121) | data formatting | bytes 1048576 | tf_op jit(solution)/shard_map/squeeze | solution.py:97
  (97 shorter events, 22.8 us)
Async XLA Ops:
  0.6 3.4 %copy-start = (bf16[128,512]{1,0:T(8,128)(2,1)S(1)}, bf16[128,512]{1,0:T(8,128)(2,1)}, u32[]{:S(2)}) copy-start(bf16[128,512]{1,0:T(8,128)(2,1)} %param.13) | copy-start | bytes 393220
  2.5 4.7 %copy-start.8 = (f32[32,32]{1,0:T(8,128)}, f32[32,32]{1,0:T(8,128)S(1)}, u32[]{:S(2)}) copy-start(f32[32,32]{1,0:T(8,128)S(1)} %broadcast_multiply_fusion.6) | copy-start | bytes 12292
  3.9 3.3 %copy-start.11 = (f32[32,32]{1,0:T(8,128)}, f32[32,32]{1,0:T(8,128)S(1)}, u32[]{:S(2)}) copy-start(f32[32,32]{1,0:T(8,128)S(1)} %add_rsqrt_fusion.1) | copy-start | bytes 12292
  4.1 3.2 %copy-start.14 = (f32[32,32]{1,0:T(8,128)}, f32[32,32]{1,0:T(8,128)S(1)}, u32[]{:S(2)}) copy-start(f32[32,32]{1,0:T(8,128)S(1)} %broadcast_multiply_fusion) | copy-start | bytes 12292
  5.5 1.4 copy-start.1
  37.0 24.6 %all-to-all-start.1 = ((bf16[16,2,32,256]{3,2,1,0:T(8,128)(2,1)}), bf16[16,2,32,256]{3,2,1,0:T(8,128)(2,1)S(1)}, u32[]{:S(2)}, u32[]{:S(2)}) async-start(bf16[16,2,32,256]{3,2,1,0:T(8,128)(2,1)} %bitcast.8), calls=%async_computation.1 | async-start | bytes 1048576 | tf_op jit(solution)/shard_map/all_to_all | solution.py:32
  62.1 11.2 %collective-permute-start = (f32[512,256]{1,0:T(8,128)S(1)}, f32[512,256]{1,0:T(8,128)S(1)}, u32[]{:S(2)}, u32[]{:S(2)}) collective-permute-start(f32[512,256]{1,0:T(8,128)S(1)} %constant_dynamic-slice_fusion), channel_id=1, source_target_pairs={{0,16},{16,0},{32,48},{48,32},{64,80},{80,64},{96,112},{112,96},{1... | collective-permute-start | bytes 1572872 | tf_op jit(solution)/shard_map/ppermute | solution.py:76
  112.4 2.4 %copy-start.7 = (f32[32,32]{1,0:T(8,128)S(1)}, f32[32,32]{1,0:T(8,128)}, u32[]{:S(2)}) copy-start(f32[32,32]{1,0:T(8,128)} %add_rsqrt_fusion) | copy-start | bytes 12292
  112.4 2.4 %copy-start.16 = (bf16[128,128]{1,0:T(8,128)(2,1)S(1)}, bf16[128,128]{1,0:T(8,128)(2,1)}, u32[]{:S(2)}) copy-start(bf16[128,128]{1,0:T(8,128)(2,1)} %param.14) | copy-start | bytes 98308
  112.4 2.4 %copy-start.18 = (f32[128]{0:T(128)S(1)}, f32[128]{0:T(128)}, u32[]{:S(2)}) copy-start(f32[128]{0:T(128)} %param.18) | copy-start | bytes 1540
  112.4 2.4 %copy-start.19 = (f32[128]{0:T(128)S(1)}, f32[128]{0:T(128)}, u32[]{:S(2)}) copy-start(f32[128]{0:T(128)} %param.19) | copy-start | bytes 1540
  112.4 2.9 %copy-start.3 = (bf16[32,32,128]{2,1,0:T(8,128)(2,1)S(1)}, bf16[32,32,128]{2,1,0:T(8,128)(2,1)}, u32[]{:S(2)}) copy-start(bf16[32,32,128]{2,1,0:T(8,128)(2,1)} %param.10) | copy-start | bytes 786436
  112.5 2.9 %copy-start.9 = (f32[32,32]{1,0:T(8,128)S(1)}, f32[32,32]{1,0:T(8,128)}, u32[]{:S(2)}) copy-start(f32[32,32]{1,0:T(8,128)} %copy-done.8) | copy-start | bytes 12292
  112.5 2.9 %copy-start.12 = (f32[32,32]{1,0:T(8,128)S(1)}, f32[32,32]{1,0:T(8,128)}, u32[]{:S(2)}) copy-start(f32[32,32]{1,0:T(8,128)} %copy-done.11) | copy-start | bytes 12292
  112.5 2.9 %copy-start.17 = (bf16[128,128]{1,0:T(8,128)(2,1)S(1)}, bf16[128,128]{1,0:T(8,128)(2,1)}, u32[]{:S(2)}) copy-start(bf16[128,128]{1,0:T(8,128)(2,1)} %param.15) | copy-start | bytes 98308
  112.5 2.9 %copy-start.20 = (f32[128]{0:T(128)S(1)}, f32[128]{0:T(128)}, u32[]{:S(2)}) copy-start(f32[128]{0:T(128)} %param.17) | copy-start | bytes 1540
  112.5 2.9 %copy-start.21 = (f32[128]{0:T(128)S(1)}, f32[128]{0:T(128)}, u32[]{:S(2)}) copy-start(f32[128]{0:T(128)} %param.16) | copy-start | bytes 1540
  114.8 1.7 copy-start.5
  116.5 0.8 copy-start.4
  146.8 5.8 %collective-permute-start.1 = (bf16[512,256]{1,0:T(8,128)(2,1)S(1)}, bf16[512,256]{1,0:T(8,128)(2,1)S(1)}, u32[]{:S(2)}, u32[]{:S(2)}) collective-permute-start(bf16[512,256]{1,0:T(8,128)(2,1)S(1)} %bitcast.142), channel_id=1, source_target_pairs={{0,16},{16,0},{32,48},{48,32},{64,80},{80,64},{96,112},{112,96},{1... | collective-permute-start | bytes 786440 | tf_op jit(solution)/shard_map/ppermute | solution.py:89
  179.5 16.9 %all-to-all-start.7 = ((bf16[16,2,8192]{2,1,0:T(2,128)(2,1)}), bf16[16,2,8192]{2,1,0:T(2,128)(2,1)S(1)}, u32[]{:S(2)}, u32[]{:S(2)}) async-start(bf16[16,2,8192]{2,1,0:T(2,128)(2,1)} %reshape.164), calls=%async_computation.7 | async-start | bytes 1048576 | tf_op jit(solution)/shard_map/all_to_all | solution.py:45
  211.3 2.3 %copy-start.2 = (f32[32,32,512]{2,1,0:T(8,128)S(1)}, f32[32,32,512]{2,1,0:T(8,128)}, u32[]{:S(2)}) copy-start(f32[32,32,512]{2,1,0:T(8,128)} %copy-done.1) | copy-start | bytes 6291460
  211.3 2.3 %copy-start.15 = (f32[32,32]{1,0:T(8,128)S(1)}, f32[32,32]{1,0:T(8,128)}, u32[]{:S(2)}) copy-start(f32[32,32]{1,0:T(8,128)} %copy-done.14) | copy-start | bytes 12292
  213.6 1.0 copy-start.6
  213.7 1.0 copy-start.10
  213.7 1.0 copy-start.13
  213.7 1.0 copy-start.22

commit v2 on v0

v2 whole, which is shorter than its diff:
```python
import jax
import jax.numpy as jnp
from jax import lax
from jax.experimental import pallas as pl
from jax.experimental.pallas import tpu as pltpu
from jax.sharding import PartitionSpec as P

epsilon = 1e-05
MESH = pl.DeviceIdType.MESH
F32 = jnp.float32
BF16 = jnp.bfloat16

PLANE = 16
DEPTH = 8
U = 8
G = 4
TILE = 32
LANES = 128
CHAN = 128
WIDE = 256


def dot(a, b):
    return lax.dot_general(a, b, (((1,), (0,)), ((), ())), preferred_element_type=F32)


def dot_nt(a, b):
    return lax.dot_general(a, b, (((1,), (1,)), ((), ())), preferred_element_type=F32)


def dot_tn(a, b):
    return lax.dot_general(a, b, (((0,), (0,)), ((), ())), preferred_element_type=F32)


def swap_groups(parts, lane):
    low = lane < 64
    even = (lane // 32) % 2 == 0
    half = [[None, None], [None, None]]
    for bit in range(2):
        a, b = parts[bit], parts[2 + bit]
        half[0][bit] = jnp.where(low, a, pltpu.roll(b, 64, 1))
        half[1][bit] = jnp.where(low, pltpu.roll(a, 64, 1), b)
    out = []
    for bit in range(2):
        a, b = half[bit]
        out.append(jnp.where(even, a, pltpu.roll(b, 32, 1)))
        out.append(jnp.where(even, pltpu.roll(a, 96, 1), b))
    return out


def plane_index(x_hi, zh, p):
    return x_hi * 8 + ((p % 2) * 2 + zh) * 2 + p // 2


def kernel(
    pair_ref, mask_ref, cot_ref, w_in_ref, w_out_ref, w_gout_ref,
    gain_in_ref, bias_in_ref, gain_out_ref, bias_out_ref,
    out_ref, grad_ref,
    w_in_t, w_out_t, w_gout_t, masks, normed_s, scaled_s, inv_s,
    proj_s, gate_s, ogate_s, cot_s, oproj_s, ggate_s,
    stage,
    ps, pr, zs, zr, us, ur,
    swap_s, swap_r, gother,
    psend, precv, zsend, zrecv, csend, crecv,
):
    row = lax.axis_index("row")
    col = lax.axis_index("col")
    z = row % 8
    x_hi = row // 8
    core = col % 2
    me = x_hi * 8 + col // 2

    def plane_peer(d):
        peer = (me + d) % PLANE
        return peer, ((peer // 8) * 8 + z, (peer % 8) * 2 + core)

    def depth_peer(d):
        peer = (z + d) % DEPTH
        return peer, (x_hi * 8 + peer, col)

    partner = (row, col + 1 - 2 * core)

    barrier = pltpu.get_barrier_semaphore()

    @pl.loop(1, PLANE)
    def _(d):
        pl.semaphore_signal(barrier, inc=1, device_id=plane_peer(d)[1], device_id_type=MESH)

    @pl.loop(1, DEPTH)
    def _(d):
        pl.semaphore_signal(barrier, inc=1, device_id=depth_peer(d)[1], device_id_type=MESH)

    pl.semaphore_signal(barrier, inc=1, device_id=partner, device_id_type=MESH)

    def rows64(index):
        return pl.ds(pl.multiple_of(index * 64, 64), 64)

    def plane_copy(t, d):
        peer, where = plane_peer(d)
        return pltpu.make_async_remote_copy(
            src_ref=ps.at[t, rows64(peer)],
            dst_ref=pr.at[t, rows64(me)],
            send_sem=psend.at[t, d],
            recv_sem=precv.at[t, d],
            device_id=where,
            device_id_type=MESH,
        )

    def depth_copy(t, d, split):
        peer, where = depth_peer(d)
        if t == 1:
            source, target = peer, (z % 2) * 4 + z // 2
        elif t == 5:
            source, target = (peer % 2) * 4 + peer // 2, z
        else:
            source, target = peer, z
        return pltpu.make_async_remote_copy(
            src_ref=zs.at[t, source],
            dst_ref=zr.at[t, target],
            send_sem=zsend.at[t, d],
            recv_sem=zrecv.at[t, d],
            device_id=where,
            device_id_type=MESH,
        )

    def plane_start(t):
        pr[t, rows64(me), :] = ps[t, rows64(me), :]

        @pl.loop(1, PLANE)
        def _(d):
            plane_copy(t, d).start()

    def plane_wait(t):
        @pl.loop(1, PLANE)
        def _(d):
            plane_copy(t, d).wait_recv()

    def depth_start(t):
        order = (z % 2) * 4 + z // 2
        if t == 1:
            zr[t, order] = zs[t, z]
        elif t == 5:
            zr[t, z] = zs[t, order]
        else:
            zr[t, z] = zs[t, z]

        @pl.loop(1, DEPTH)
        def _(d):
            depth_copy(t, d, False).start()

    def depth_wait(t):
        @pl.loop(1, DEPTH)
        def _(d):
            depth_copy(t, d, False).wait_recv()

    lane = lax.broadcasted_iota(jnp.int32, (64, LANES), 1)

    def gather_tiles(t):
        for xh in range(2):
            for zh in range(2):
                parts = [
                    pr[t, plane_index(xh, zh, p) * 64 : plane_index(xh, zh, p) * 64 + 64, :].astype(F32)
                    for p in range(4)
                ]
                moved = swap_groups(parts, lane)
                whole = jnp.concatenate([m.reshape(8, 1, U, LANES) for m in moved], axis=1)
                zs[t, :, xh * 32 : xh * 32 + 32, zh * 128 : zh * 128 + 128] = whole.reshape(
                    8, 32, LANES
                ).astype(BF16)

    def scatter_tiles(t):
        for xh in range(2):
            for zh in range(2):
                block = zr[t, :, xh * 32 : xh * 32 + 32, zh * 128 : zh * 128 + 128]
                block = block.astype(F32).reshape(8, G, U, LANES)
                parts = [block[:, g].reshape(64, LANES) for g in range(G)]
                moved = swap_groups(parts, lane)
                for p in range(4):
                    at = plane_index(xh, zh, p) * 64
                    ps[t, at : at + 64, :] = moved[p].astype(BF16)

    def strided(u):
        return pl.ds(u, CHAN, stride=U)

    w_in_t[...] = w_in_ref[...].astype(F32).T.astype(BF16)
    w_out_t[...] = w_out_ref[...].astype(F32).T.astype(BF16)
    w_gout_t[...] = w_gout_ref[...].astype(F32).T.astype(BF16)

    def column(ref):
        return jnp.broadcast_to(ref[...].reshape(1, CHAN), (8, CHAN)).T[:, 0:1]

    gain_in = column(gain_in_ref)
    bias_in = column(bias_in_ref)
    gain_out = column(gain_out_ref)
    bias_out = column(bias_out_ref)

    valid = jnp.broadcast_to(mask_ref[...].reshape(1, 512), (8, 512)).astype(F32).astype(BF16)
    number = lax.broadcasted_iota(jnp.int32, (512, LANES), 0)
    place = lax.broadcasted_iota(jnp.int32, (512, LANES), 1)
    col_pick = (number == col * TILE + place % 32).astype(F32).astype(BF16)
    col_valid = dot(valid, col_pick)

    def normalize(values, gain, bias):
        average = jnp.mean(values, axis=0, keepdims=True)
        centred = values - average
        inverse = lax.rsqrt(jnp.mean(centred * centred, axis=0, keepdims=True) + epsilon)
        scaled = centred * inverse
        return scaled * gain + bias, scaled, inverse

    def norm_back(grad, gain, scaled, inverse):
        s = grad * gain
        first = jnp.mean(s, axis=0, keepdims=True)
        second = jnp.mean(s * scaled, axis=0, keepdims=True)
        return (s - first - scaled * second) * inverse

    def tile_of(ref, u):
        rows = jnp.concatenate([ref[g * U + u] for g in range(G)], axis=0)
        return rows.astype(F32).T

    def branch(t, u, normed):
        base = t * CHAN
        projected = dot(w_in_t[base : base + CHAN, :], normed)
        gates = jax.nn.sigmoid(dot(w_in_t[2 * CHAN + base : 3 * CHAN + base, :], normed))
        mask = masks[u]
        gate_s[u, base : base + CHAN, :] = gates * mask
        value = gates * projected * mask
        proj_s[u, base : base + CHAN, :] = value * (1.0 - gates)
        stage[t, strided(u), :] = value

    @pl.loop(0, U)
    def _(u):
        row_pick = (number == row * TILE + (place // 32) * U + u).astype(F32).astype(BF16)
        masks[u] = (dot(valid, row_pick) * col_valid)[0:1, :]
        normed, scaled, inverse = normalize(tile_of(pair_ref, u), gain_in, bias_in)
        normed = normed.astype(BF16)
        normed_s[u] = normed
        scaled_s[u] = scaled
        inv_s[u] = inverse
        branch(0, u, normed)

    ps[0] = stage[0].astype(BF16)
    pl.semaphore_wait(barrier, (PLANE - 1) + (DEPTH - 1) + 1)
    plane_start(0)

    @pl.loop(0, U)
    def _(u):
        branch(1, u, normed_s[u])

    ps[1] = stage[1].astype(BF16)
    plane_start(1)

    plane_wait(0)
    gather_tiles(0)
    depth_start(0)
    plane_wait(1)
    gather_tiles(1)
    depth_start(1)

    @pl.loop(0, U)
    def _(u):
        ogate_s[u] = jax.nn.sigmoid(dot(w_gout_t[...], normed_s[u]))
        cot_s[u] = tile_of(cot_ref, u)

    depth_wait(0)
    depth_wait(1)

    left = zr[0].reshape(8 * 64, WIDE)

    def right_half(which):
        return zr[1, pl.ds(which * 4, 4)].reshape(WIDE, WIDE)

    def to_partner(i, src, dst):
        return pltpu.make_async_remote_copy(
            src_ref=src,
            dst_ref=dst,
            send_sem=csend.at[i],
            recv_sem=crecv.at[i],
            device_id=partner,
            device_id_type=MESH,
        )

    swap_s[...] = dot_nt(left, right_half(1 - core)).astype(BF16)
    tri_copy = to_partner(0, swap_s, swap_r)
    tri_copy.start()
    mine = dot_nt(left, right_half(core))
    tri_copy.wait_recv()
    zs[2] = (mine + swap_r[...].astype(F32)).astype(BF16).reshape(8, 64, WIDE)
    depth_start(2)
    depth_wait(2)
    scatter_tiles(2)
    plane_start(2)
    plane_wait(2)

    stage[2] = pr[2].astype(F32)

    @pl.loop(0, U)
    def _(u):
        tri = stage[2, strided(u), :]
        out_norm, scaled, inverse = normalize(tri, gain_out, bias_out)
        outer_proj = dot(w_out_t[...], out_norm.astype(BF16))
        outer_gate = ogate_s[u]
        upstream = cot_s[u]
        gated = upstream * outer_gate
        grad_outnorm = dot(w_out_ref[...], gated.astype(BF16))
        oproj_s[u] = outer_proj
        stage[3, strided(u), :] = norm_back(grad_outnorm, gain_out, scaled, inverse)

    ps[3] = stage[3].astype(BF16)
    plane_start(3)

    @pl.loop(0, U)
    def _(u):
        outer_proj = oproj_s[u]
        outer_gate = ogate_s[u]
        whole = (outer_gate * outer_proj).T.astype(BF16)
        for g in range(G):
            out_ref[g * U + u] = whole[g * TILE : g * TILE + TILE, :]
        grad_gate = (cot_s[u] * outer_proj * outer_gate * (1.0 - outer_gate)).astype(BF16)
        ggate_s[u] = dot(w_gout_ref[...], grad_gate)

    plane_wait(3)
    gather_tiles(3)
    depth_start(3)
    depth_wait(3)

    grad_copy = to_partner(1, zr.at[3], gother)
    grad_copy.start()
    own = zr[3].reshape(512, WIDE)
    half = dot_tn(own, left).astype(BF16).reshape(4, 64, WIDE)
    zs[5, pl.ds(core * 4, 4)] = half
    grad_left = dot(own, right_half(core))
    grad_copy.wait_recv()
    other = gother[...].reshape(512, WIDE)
    grad_left = grad_left + dot(other, right_half(1 - core))
    zs[4] = grad_left.astype(BF16).reshape(8, 64, WIDE)
    depth_start(4)
    half = dot_tn(other, left).astype(BF16).reshape(4, 64, WIDE)
    zs[5, pl.ds((1 - core) * 4, 4)] = half
    depth_start(5)
    depth_wait(4)
    scatter_tiles(4)
    plane_start(4)
    depth_wait(5)
    scatter_tiles(5)
    plane_start(5)
    plane_wait(4)
    stage[4] = pr[4].astype(F32)
    plane_wait(5)
    stage[5] = pr[5].astype(F32)

    @pl.loop(0, U)
    def _(u):
        gl = stage[4, strided(u), :]
        gr = stage[5, strided(u), :]
        mixed = jnp.concatenate(
            [
                gl * gate_s[u, 0:CHAN, :],
                gr * gate_s[u, CHAN : 2 * CHAN, :],
                gl * proj_s[u, 0:CHAN, :],
                gr * proj_s[u, CHAN : 2 * CHAN, :],
            ],
            axis=0,
        ).astype(BF16)
        grad_normed = dot(w_in_ref[...], mixed) + ggate_s[u]
        whole = norm_back(grad_normed, gain_in, scaled_s[u], inv_s[u]).T.astype(BF16)
        for g in range(G):
            grad_ref[g * U + u] = whole[g * TILE : g * TILE + TILE, :]

    for t in range(6):

        @pl.loop(1, PLANE)
        def _(d):
            plane_copy(t, d).wait_send()

        @pl.loop(1, DEPTH)
        def _(d):
            depth_copy(t, d, False).wait_send()

    tri_copy.wait_send()
    grad_copy.wait_send()


def per_device(
    pair, residue_mask, cotangent, w_in, w_out, w_gout, gain_in, bias_in, gain_out, bias_out
):
    vmem = pl.BlockSpec(memory_space=pltpu.VMEM)
    shape = jax.ShapeDtypeStruct(pair.shape, BF16)
    return pl.pallas_call(
        kernel,
        out_shape=(shape, shape),
        in_specs=[vmem] * 10,
        out_specs=(vmem, vmem),
        scratch_shapes=[
            pltpu.VMEM((4 * CHAN, CHAN), BF16),
            pltpu.VMEM((CHAN, CHAN), BF16),
            pltpu.VMEM((CHAN, CHAN), BF16),
            pltpu.VMEM((U, 1, LANES), F32),
            pltpu.VMEM((U, CHAN, LANES), BF16),
            pltpu.VMEM((U, CHAN, LANES), F32),
            pltpu.VMEM((U, 1, LANES), F32),
            pltpu.VMEM((U, 2 * CHAN, LANES), F32),
            pltpu.VMEM((U, 2 * CHAN, LANES), F32),
            pltpu.VMEM((U, CHAN, LANES), F32),
            pltpu.VMEM((U, CHAN, LANES), F32),
            pltpu.VMEM((U, CHAN, LANES), F32),
            pltpu.VMEM((U, CHAN, LANES), F32),
            pltpu.VMEM((6, CHAN * U, LANES), F32),
            pltpu.VMEM((6, CHAN * U, LANES), BF16),
            pltpu.VMEM((6, CHAN * U, LANES), BF16),
            pltpu.VMEM((6, DEPTH, 64, WIDE), BF16),
            pltpu.VMEM((6, DEPTH, 64, WIDE), BF16),
            pltpu.VMEM((8, LANES), F32),
            pltpu.VMEM((8, LANES), F32),
            pltpu.VMEM((512, WIDE), BF16),
            pltpu.VMEM((512, WIDE), BF16),
            pltpu.VMEM((DEPTH, 64, WIDE), BF16),
            pltpu.SemaphoreType.DMA((6, PLANE)),
            pltpu.SemaphoreType.DMA((6, PLANE)),
            pltpu.SemaphoreType.DMA((6, DEPTH)),
            pltpu.SemaphoreType.DMA((6, DEPTH)),
            pltpu.SemaphoreType.DMA((2,)),
            pltpu.SemaphoreType.DMA((2,)),
        ],
        compiler_params=pltpu.CompilerParams(
            collective_id=0, has_side_effects=True, vmem_limit_bytes=48 * 1024 * 1024
        ),
    )(pair, residue_mask, cotangent, w_in, w_out, w_gout, gain_in, bias_in, gain_out, bias_out)


def solution(mesh):
    tile = P("row", "col", None)
    return jax.shard_map(
        per_device,
        mesh=mesh,
        in_specs=(tile, P(), tile, P(), P(), P(), P(), P(), P(), P()),
        out_specs=(tile, tile),
        check_vma=False,
    )
```

time: 639 us -> 100 us (0.16)
  waiting for transfers between devices: 442 us -> 0 us
  blocking collectives: 94.5 us -> 0 us
  Pallas kernels: 0 us -> 90.2 us
  local copies, waits for them, and re-layouts: 45.2 us -> 9.02 us
  matrix products: 27.2 us -> 0 us
  between operations: 14 us -> 0.66 us
  other arithmetic: 10.3 us -> 0 us
    reduce_scatter x2 -> x0, waiting for transfers between devices: 199 us -> none  [the longest x1 199 us: per_device(): lax.psum_scatter(moved.astype(jnp.bfloat16), 'row', scatter_dimension=0,...]
    psum x1 -> x0, waiting for transfers between devices: 159 us -> none  [from_root(): return lax.psum(kept, axis)]
    all_to_all x1 -> x0, blocking collectives: 94.5 us -> none  [per_device(): lax.all_to_all(partial_right.astype(jnp.bfloat16), 'col', split_axis=1, c...]
    pallas_call x0 -> x1, Pallas kernels: none -> 90.2 us  [per_device(): pl.pallas_call(kernel, out_shape=(shape, shape), in_specs=[vmem] * 10, ou...]
    all_gather x2 -> x0, waiting for transfers between devices: 83.6 us -> none  [the longest x1 43.5 us: per_device(): lax.all_gather(right, 'col', axis=1, tiled=True)]
    dot_general x9 -> x0, matrix products: 27.2 us -> none  [the longest x1 6.07 us: per_device(): jnp.einsum('ikc,jkc->ijc', left_panel, received, preferred_element_type=j...]
    convert_element_type x2 -> x0, local copies, waits for them, and re-layouts: 11.8 us -> none  [the longest x1 9.12 us: per_device(): partial_right.astype(jnp.bfloat16)]
    dot_general x2 -> x0, local copies, waits for them, and re-layouts: 10.7 us -> none  [the longest x1 7.89 us: per_device(): jnp.einsum('ijc,jkc->kic', grad_tri, received, preferred_element_type=jnp...]
  transfers between devices with their start and end apart: 5 -> 0, of which waited for: 4 -> 0; matrix products, arithmetic and copies ran while one was open for 5% -> 0% of each run, Pallas kernels for 0% -> 0%
where the time goes in v2:
time: 100 us; the launch traced here: 99.8 us
  Pallas kernels  90.2 us (90%)
  local copies, waits for them, and re-layouts  9.02 us (9%)
    pallas_call x1, Pallas kernels, per_device(): pl.pallas_call(kernel, out_shape=(shape, shape), in_specs=[vmem] * 10, ou...  90.2 us
    unnamed x22, local copies, waits for them, and re-layouts  9.02 us

profile of v2, /device:TPU:1, one launch (start us, length us, event | category | flops | bytes accessed | tf_op | source)
XLA Modules:
  0.0 99.8 jit_solution(2811600516641334892)
XLA Ops:
  0.6 0.0 copy-start
  0.6 0.9 copy-done
  1.6 0.0 copy-start.1
  1.6 0.9 copy-done.1
  2.5 0.0 copy-start.2
  2.5 0.9 copy-done.2
  3.4 0.0 copy-start.3
  3.4 0.8 copy-done.3
  4.2 0.0 copy-start.4
  4.2 0.8 copy-done.4
  5.0 0.0 copy-start.5
  5.0 0.7 copy-done.5
  5.6 0.0 copy-start.6
  5.6 0.7 copy-done.6
  6.3 0.0 copy-start.7
  6.3 0.7 copy-done.7
  7.0 0.0 copy-start.8
  7.0 0.7 copy-done.8
  7.6 0.0 copy-start.9
  7.6 0.7 copy-done.9
  8.3 90.2 %shard_map.113 = (bf16[32,32,128]{2,1,0:T(8,128)(2,1)S(1)}, bf16[32,32,128]{2,1,0:T(8,128)(2,1)S(1)}) custom-call(bf16[32,32,128]{2,1,0:T(8,128)(2,1)S(1)} %copy-done, s32[512]{0:T(512)S(1)} %copy-done.5, bf16[32,32,128]{2,1,0:T(8,128)(2,1)S(1)} %copy-done.1, bf16[128,512]{1,0:T(8,128)(2,1)S(1)} %copy-done.2, bf16[128,128]{1,0:T(8,128)(2,1)S(1)} %copy-done.3, ...), custom_call_target="tpu_custom_call" | custom-call | tf_op jit(solution)/shard_map/pallas_call | solution.py:388
  98.4 0.7 copy.14
  99.1 0.7 copy.15
Async XLA Ops:
  0.6 1.0 copy-start
  1.6 0.9 copy-start.1
  2.5 0.9 copy-start.2
  3.4 0.8 copy-start.3
  4.2 0.8 copy-start.4
  5.0 0.7 copy-start.5
  5.6 0.7 copy-start.6
  6.3 0.7 copy-start.7
  7.0 0.7 copy-start.8
  7.6 0.7 copy-start.9

commit v3 on v0

v3 whole, which is shorter than its diff:
```python
import jax
import jax.numpy as jnp
from jax import lax
from jax.experimental import pallas as pl
from jax.experimental.pallas import tpu as pltpu
from jax.sharding import PartitionSpec as P

epsilon = 1e-05
MESH = pl.DeviceIdType.MESH
F32 = jnp.float32
BF16 = jnp.bfloat16

U = 8
G = 4
V = 4
TILE = 32
LANES = 128
CHAN = 128
WIDE = 256
Q = 8


def dot(a, b):
    return lax.dot_general(a, b, (((1,), (0,)), ((), ())), preferred_element_type=F32)


def dot_nt(a, b):
    return lax.dot_general(a, b, (((1,), (1,)), ((), ())), preferred_element_type=F32)


def dot_tn(a, b):
    return lax.dot_general(a, b, (((0,), (0,)), ((), ())), preferred_element_type=F32)


def swap_groups(parts):
    lane = lax.broadcasted_iota(jnp.int32, parts[0].shape, 1)
    low = lane < 64
    even = (lane // 32) % 2 == 0
    half = [[None, None], [None, None]]
    for bit in range(2):
        a, b = parts[bit], parts[2 + bit]
        half[0][bit] = jnp.where(low, a, pltpu.roll(b, 64, 1))
        half[1][bit] = jnp.where(low, pltpu.roll(a, 64, 1), b)
    out = []
    for bit in range(2):
        a, b = half[bit]
        out.append(jnp.where(even, a, pltpu.roll(b, 32, 1)))
        out.append(jnp.where(even, pltpu.roll(a, 96, 1), b))
    return out


def normalize(values, gain, bias):
    average = jnp.mean(values, axis=0, keepdims=True)
    centred = values - average
    inverse = lax.rsqrt(jnp.mean(centred * centred, axis=0, keepdims=True) + epsilon)
    scaled = centred * inverse
    return scaled * gain + bias, scaled, inverse


def norm_back(grad, gain, scaled, inverse):
    s = grad * gain
    first = jnp.mean(s, axis=0, keepdims=True)
    second = jnp.mean(s * scaled, axis=0, keepdims=True)
    return (s - first - scaled * second) * inverse


def tile_of(ref, v):
    rows = [ref[g * U + 2 * v + e] for e in range(2) for g in range(G)]
    return jnp.concatenate(rows, axis=0).astype(F32).T


def store_tile(ref, v, values):
    whole = values.T.astype(BF16)
    for e in range(2):
        for g in range(G):
            at = (e * G + g) * TILE
            ref[g * U + 2 * v + e] = whole[at : at + TILE, :]


def kernel(
    pair_hbm, mask_hbm, cot_hbm, w_in_hbm, w_out_hbm, w_gout_hbm,
    gain_in_hbm, bias_in_hbm, gain_out_hbm, bias_out_hbm,
    out_hbm, grad_hbm,
    pair_ref, mask_ref, cot_ref, w_in_ref, w_out_ref, w_gout_ref,
    gain_in_ref, bias_in_ref, gain_out_ref, bias_out_ref,
    out_ref, grad_ref,
    w_in_t, w_out_t, w_gout_t, masks, normed_s, scaled_s, inv_s,
    proj_s, gate_s, ogate_s, cot_s, oproj_s, ggate_s,
    stage, sx, rx, left_m, right_m, own_m, other_m, swap_s, swap_r,
    send_sem, recv_sem, csend, crecv, local_sem, ready_sem,
):
    arrays = [
        (pair_hbm, pair_ref), (mask_hbm, mask_ref), (w_in_hbm, w_in_ref), (w_out_hbm, w_out_ref),
        (w_gout_hbm, w_gout_ref), (gain_in_hbm, gain_in_ref), (bias_in_hbm, bias_in_ref),
        (gain_out_hbm, gain_out_ref), (bias_out_hbm, bias_out_ref), (cot_hbm, cot_ref),
    ]
    loads = [
        pltpu.make_async_copy(src, dst, local_sem.at[i]) for i, (src, dst) in enumerate(arrays)
    ]
    for load in loads:
        load.start()
    store_out = pltpu.make_async_copy(out_ref, out_hbm, local_sem.at[10])
    store_grad = pltpu.make_async_copy(grad_ref, grad_hbm, local_sem.at[11])

    row = lax.axis_index("row")
    col = lax.axis_index("col")
    z = row % 8
    x_hi = row // 8
    core = col % 2
    q = col // 2
    partner = (row, col + 1 - 2 * core)

    barrier = pltpu.get_barrier_semaphore()

    def depth_peer(d):
        return (x_hi * 8 + (z + d) % 8, col)

    @pl.loop(1, 16)
    def _(d):
        peer = (x_hi * 8 + q + d) % 16
        where = ((peer // 8) * 8 + z, (peer % 8) * 2 + core)
        pl.semaphore_signal(barrier, inc=1, device_id=where, device_id_type=MESH)

    @pl.loop(1, 8)
    def _(d):
        pl.semaphore_signal(barrier, inc=1, device_id=depth_peer(d), device_id_type=MESH)

    pl.semaphore_signal(barrier, inc=1, device_id=partner, device_id_type=MESH)

    def post(t, to_row, to_q):
        return pltpu.make_async_remote_copy(
            src_ref=sx.at[t, to_row // 2, to_row % 2, to_q],
            dst_ref=rx.at[t, row // 2, row % 2, q],
            send_sem=send_sem.at[t],
            recv_sem=recv_sem.at[t],
            device_id=(to_row, to_q * 2 + core),
            device_id_type=MESH,
        )

    def keep(t):
        pltpu.make_async_copy(
            sx.at[t, row // 2, row % 2, q], rx.at[t, row // 2, row % 2, q], recv_sem.at[t]
        ).start()

    def send(t):
        keep(t)

        @pl.loop(1, 128)
        def _(d):
            to = (row * 8 + q + d) % 128
            post(t, to // 8, to % 8).start()

    def send_rows(t, parity):
        same = row % 2 == parity

        @pl.when(same)
        def _():
            keep(t)

        @pl.when(jnp.logical_not(same))
        def _():
            post(t, (row // 2) * 2 + parity, q).start()

        @pl.loop(1, 64)
        def _(d):
            to = ((row // 2) * 8 + q + d) % 64
            post(t, (to // 8) * 2 + parity, to % 8).start()

    def receive(t):
        pltpu.make_async_copy(sx.at[t], rx.at[t], recv_sem.at[t]).wait()

    def sent(t):
        for part in (sx.at[t, pl.ds(0, 7)], sx.at[t, 7, 0], sx.at[t, 7, 1, pl.ds(0, 7)]):
            pltpu.make_async_copy(part, part, send_sem.at[t]).wait()

    def gather(t, half):
        parts = [rx[t, :, :, half * 4 + p].astype(F32).reshape(16 * U, LANES) for p in range(4)]
        moved = [m.reshape(16, 1, U, LANES) for m in swap_groups(parts)]
        return jnp.concatenate(moved, axis=1).reshape(512, LANES).astype(BF16)

    def scatter(t, block, half, parity=None):
        rows = block.shape[0] // TILE
        block = block.reshape(rows, G, U, LANES)
        parts = [block[:, g].reshape(rows * U, LANES) for g in range(G)]
        for p, moved in enumerate(swap_groups(parts)):
            if parity is None:
                sx[t, :, :, half * 4 + p] = moved.reshape(8, 2, U, LANES).astype(BF16)
            else:
                sx[t, :, parity, half * 4 + p] = moved.reshape(8, U, LANES).astype(BF16)

    def halves(x):
        return [x[:, 0:LANES], x[:, LANES : 2 * LANES]]

    def strided(v, e):
        return pl.ds(2 * v + e, CHAN, stride=U)

    def put(t, v, values):
        for e, value in enumerate(halves(values)):
            stage[t, strided(v, e), :] = value

    def get(t, v):
        return jnp.concatenate([stage[t, strided(v, e), :] for e in range(2)], axis=1)

    def pack(t):
        sx[t] = stage[t].reshape(8, 2, Q, U, LANES).astype(BF16)

    def unpack(t):
        stage[t] = rx[t].astype(F32).reshape(CHAN * U, LANES)

    for load in loads[1:9]:
        load.wait()
    w_in_t[...] = w_in_ref[...].astype(F32).T.astype(BF16)
    w_out_t[...] = w_out_ref[...].astype(F32).T.astype(BF16)
    w_gout_t[...] = w_gout_ref[...].astype(F32).T.astype(BF16)

    def column(ref):
        return jnp.broadcast_to(ref[...].reshape(1, CHAN), (8, CHAN)).T[:, 0:1]

    gain_in = column(gain_in_ref)
    bias_in = column(bias_in_ref)
    gain_out = column(gain_out_ref)
    bias_out = column(bias_out_ref)

    valid = jnp.broadcast_to(mask_ref[...].reshape(1, 512), (8, 512)).astype(F32).astype(BF16)
    number = lax.broadcasted_iota(jnp.int32, (512, WIDE), 0)
    place = lax.broadcasted_iota(jnp.int32, (512, WIDE), 1)
    col_pick = (number == col * TILE + place % 32).astype(F32).astype(BF16)
    col_valid = dot(valid, col_pick)
    for v in range(V):
        first = row * TILE + ((place // 32) % G) * U + place // LANES + 2 * v
        row_pick = (number == first).astype(F32).astype(BF16)
        masks[v] = (dot(valid, row_pick) * col_valid)[0:1, :]

    def branch(t, v, normed):
        base = t * CHAN
        projected = dot(w_in_t[base : base + CHAN, :], normed)
        gates = jax.nn.sigmoid(dot(w_in_t[2 * CHAN + base : 3 * CHAN + base, :], normed))
        mask = masks[v]
        gate_s[v, base : base + CHAN, :] = gates * mask
        value = gates * projected * mask
        proj_s[v, base : base + CHAN, :] = value * (1.0 - gates)
        put(t, v, value)

    loads[0].wait()

    @pl.loop(0, V)
    def _(v):
        normed, scaled, inverse = normalize(tile_of(pair_ref, v), gain_in, bias_in)
        normed = normed.astype(BF16)
        normed_s[v] = normed
        scaled_s[v] = scaled
        inv_s[v] = inverse
        branch(1, v, normed)

    pack(1)
    pl.semaphore_wait(barrier, 15 + 7 + 1)

    @pl.loop(1, 8)
    def _(d):
        pl.semaphore_signal(ready_sem, inc=1, device_id=depth_peer(d), device_id_type=MESH)

    pl.semaphore_wait(ready_sem, 7)
    send(1)

    @pl.loop(0, V)
    def _(v):
        branch(0, v, normed_s[v])

    pack(0)
    send(0)

    loads[9].wait()

    @pl.loop(0, V)
    def _(v):
        ogate_s[v] = jax.nn.sigmoid(dot(w_gout_t[...], normed_s[v]))
        cot_s[v] = tile_of(cot_ref, v)

    receive(1)
    for half in range(2):
        whole = gather(1, half).reshape(8, 2, TILE, LANES)
        for side in range(2):
            right_m[side, :, half * LANES : half * LANES + LANES] = whole[:, side].reshape(WIDE, LANES)

    receive(0)
    for half in range(2):
        left_m[:, half * LANES : half * LANES + LANES] = gather(0, half)

    def to_partner(i, src, dst):
        return pltpu.make_async_remote_copy(
            src_ref=src,
            dst_ref=dst,
            send_sem=csend.at[i],
            recv_sem=crecv.at[i],
            device_id=partner,
            device_id_type=MESH,
        )

    swap_s[...] = dot_nt(left_m[...], right_m[1 - core]).astype(BF16)
    tri_copy = to_partner(0, swap_s, swap_r)
    tri_copy.start()
    mine = dot_nt(left_m[...], right_m[core])
    tri_copy.wait_recv()
    mine = mine + swap_r[...].astype(F32)
    for half in range(2):
        scatter(2, halves(mine)[half], half)
    send(2)
    receive(2)

    unpack(2)

    @pl.loop(0, V)
    def _(v):
        out_norm, scaled, inverse = normalize(get(2, v), gain_out, bias_out)
        outer_proj = dot(w_out_t[...], out_norm.astype(BF16))
        gated = cot_s[v] * ogate_s[v]
        grad_outnorm = dot(w_out_ref[...], gated.astype(BF16))
        oproj_s[v] = outer_proj
        put(3, v, norm_back(grad_outnorm, gain_out, scaled, inverse))

    pack(3)
    send(3)

    @pl.loop(0, V)
    def _(v):
        outer_proj = oproj_s[v]
        outer_gate = ogate_s[v]
        store_tile(out_ref, v, outer_gate * outer_proj)
        grad_gate = (cot_s[v] * outer_proj * outer_gate * (1.0 - outer_gate)).astype(BF16)
        ggate_s[v] = dot(w_gout_ref[...], grad_gate)

    store_out.start()
    receive(3)

    for half in range(2):
        own_m[:, half * LANES : half * LANES + LANES] = gather(3, half)
    grad_copy = to_partner(1, own_m, other_m)
    grad_copy.start()
    grad_right = dot_tn(own_m[...], left_m[...])
    for half in range(2):
        scatter(5, halves(grad_right)[half], half, core)
    send_rows(5, core)
    grad_left = dot(own_m[...], right_m[core])
    grad_copy.wait_recv()
    grad_left = grad_left + dot(other_m[...], right_m[1 - core])
    for half in range(2):
        scatter(4, halves(grad_left)[half], half)
    send(4)
    grad_right = dot_tn(other_m[...], left_m[...])
    for half in range(2):
        scatter(5, halves(grad_right)[half], half, 1 - core)
    send_rows(5, 1 - core)
    receive(4)
    unpack(4)
    receive(5)
    unpack(5)

    @pl.loop(0, V)
    def _(v):
        gl = get(4, v)
        gr = get(5, v)
        mixed = jnp.concatenate(
            [
                gl * gate_s[v, 0:CHAN, :],
                gr * gate_s[v, CHAN : 2 * CHAN, :],
                gl * proj_s[v, 0:CHAN, :],
                gr * proj_s[v, CHAN : 2 * CHAN, :],
            ],
            axis=0,
        ).astype(BF16)
        grad_normed = dot(w_in_ref[...], mixed) + ggate_s[v]
        store_tile(grad_ref, v, norm_back(grad_normed, gain_in, scaled_s[v], inv_s[v]))

    store_grad.start()
    for t in range(6):
        sent(t)
    tri_copy.wait_send()
    grad_copy.wait_send()
    store_out.wait()
    store_grad.wait()


def per_device(
    pair, residue_mask, cotangent, w_in, w_out, w_gout, gain_in, bias_in, gain_out, bias_out
):
    hbm = pl.BlockSpec(memory_space=pl.ANY)
    shape = jax.ShapeDtypeStruct(pair.shape, BF16)
    args = (
        pair, residue_mask, cotangent, w_in, w_out, w_gout, gain_in, bias_in, gain_out, bias_out
    )
    return pl.pallas_call(
        kernel,
        out_shape=(shape, shape),
        in_specs=[hbm] * 10,
        out_specs=(hbm, hbm),
        scratch_shapes=[pltpu.VMEM(a.shape, a.dtype) for a in args]
        + [
            pltpu.VMEM(pair.shape, BF16),
            pltpu.VMEM(pair.shape, BF16),
            pltpu.VMEM((4 * CHAN, CHAN), BF16),
            pltpu.VMEM((CHAN, CHAN), BF16),
            pltpu.VMEM((CHAN, CHAN), BF16),
            pltpu.VMEM((V, 1, WIDE), F32),
            pltpu.VMEM((V, CHAN, WIDE), BF16),
            pltpu.VMEM((V, CHAN, WIDE), F32),
            pltpu.VMEM((V, 1, WIDE), F32),
            pltpu.VMEM((V, 2 * CHAN, WIDE), F32),
            pltpu.VMEM((V, 2 * CHAN, WIDE), F32),
            pltpu.VMEM((V, CHAN, WIDE), F32),
            pltpu.VMEM((V, CHAN, WIDE), F32),
            pltpu.VMEM((V, CHAN, WIDE), F32),
            pltpu.VMEM((V, CHAN, WIDE), F32),
            pltpu.VMEM((6, CHAN * U, LANES), F32),
            pltpu.VMEM((6, 8, 2, Q, U, LANES), BF16),
            pltpu.VMEM((6, 8, 2, Q, U, LANES), BF16),
            pltpu.VMEM((512, WIDE), BF16),
            pltpu.VMEM((2, WIDE, WIDE), BF16),
            pltpu.VMEM((512, WIDE), BF16),
            pltpu.VMEM((512, WIDE), BF16),
            pltpu.VMEM((512, WIDE), BF16),
            pltpu.VMEM((512, WIDE), BF16),
            pltpu.SemaphoreType.DMA((6,)),
            pltpu.SemaphoreType.DMA((6,)),
            pltpu.SemaphoreType.DMA((2,)),
            pltpu.SemaphoreType.DMA((2,)),
            pltpu.SemaphoreType.DMA((12,)),
            pltpu.SemaphoreType.REGULAR,
        ],
        compiler_params=pltpu.CompilerParams(
            collective_id=0, has_side_effects=True, vmem_limit_bytes=60 * 1024 * 1024
        ),
    )(*args)


def solution(mesh):
    tile = P("row", "col", None)
    return jax.shard_map(
        per_device,
        mesh=mesh,
        in_specs=(tile, P(), tile, P(), P(), P(), P(), P(), P(), P()),
        out_specs=(tile, tile),
        check_vma=False,
    )
```

time: 639 us -> 76.7 us (0.12)
  waiting for transfers between devices: 442 us -> 0 us
  blocking collectives: 94.5 us -> 0 us
  Pallas kernels: 0 us -> 73.5 us
  local copies, waits for them, and re-layouts: 45.2 us -> 2.42 us
  matrix products: 27.2 us -> 0 us
  between operations: 14 us -> 0.65 us
  other arithmetic: 10.3 us -> 0 us
    reduce_scatter x2 -> x0, waiting for transfers between devices: 199 us -> none  [the longest x1 199 us: per_device(): lax.psum_scatter(moved.astype(jnp.bfloat16), 'row', scatter_dimension=0,...]
    psum x1 -> x0, waiting for transfers between devices: 159 us -> none  [from_root(): return lax.psum(kept, axis)]
    all_to_all x1 -> x0, blocking collectives: 94.5 us -> none  [per_device(): lax.all_to_all(partial_right.astype(jnp.bfloat16), 'col', split_axis=1, c...]
    all_gather x2 -> x0, waiting for transfers between devices: 83.6 us -> none  [the longest x1 43.5 us: per_device(): lax.all_gather(right, 'col', axis=1, tiled=True)]
    pallas_call x0 -> x1, Pallas kernels: none -> 73.5 us  [per_device(): pl.pallas_call(kernel, out_shape=(shape, shape), in_specs=[hbm] * 10, out...]
    dot_general x9 -> x0, matrix products: 27.2 us -> none  [the longest x1 6.07 us: per_device(): jnp.einsum('ikc,jkc->ijc', left_panel, received, preferred_element_type=j...]
    convert_element_type x2 -> x0, local copies, waits for them, and re-layouts: 11.8 us -> none  [the longest x1 9.12 us: per_device(): partial_right.astype(jnp.bfloat16)]
    dot_general x2 -> x0, local copies, waits for them, and re-layouts: 10.7 us -> none  [the longest x1 7.89 us: per_device(): jnp.einsum('ijc,jkc->kic', grad_tri, received, preferred_element_type=jnp...]
  transfers between devices with their start and end apart: 5 -> 0, of which waited for: 4 -> 0; matrix products, arithmetic and copies ran while one was open for 5% -> 0% of each run, Pallas kernels for 0% -> 0%
where the time goes in v3:
time: 76.7 us; the launch traced here: 76.6 us
  Pallas kernels  73.5 us (96%)
  local copies, waits for them, and re-layouts  2.42 us (3%)
    pallas_call x1, Pallas kernels, per_device(): pl.pallas_call(kernel, out_shape=(shape, shape), in_specs=[hbm] * 10, out...  73.5 us
    unnamed x4, local copies, waits for them, and re-layouts  2.42 us

profile of v3, /device:TPU:1, one launch (start us, length us, event | category | flops | bytes accessed | tf_op | source)
XLA Modules:
  0.0 76.6 jit_solution(16682303676908494747)
XLA Ops:
  0.6 73.5 %shard_map.113 = (bf16[32,32,128]{2,1,0:T(8,128)(2,1)}, bf16[32,32,128]{2,1,0:T(8,128)(2,1)}) custom-call(bf16[32,32,128]{2,1,0:T(8,128)(2,1)} %pair_hbm.1, s32[512]{0:T(512)} %mask_hbm.1, bf16[32,32,128]{2,1,0:T(8,128)(2,1)} %cot_hbm.1, bf16[128,512]{1,0:T(8,128)(2,1)} %w_in_hbm.1, bf16[128,128]{1,0:T(8,128)(2,1)} %w_out_hbm.1, ...), custom_call_target="tpu_custom_call" | custom-call | tf_op jit(solution)/shard_map/pallas_call | solution.py:391
  74.1 0.0 copy-start
  74.1 1.7 %copy.14 = bf16[32,32,128]{2,1,0:T(8,128)(2,1)} copy(bf16[32,32,128]{2,1,0:T(8,128)(2,1)} %get-tuple-element.4) | data formatting | bytes 524288
  75.8 0.0 copy-done
  75.8 0.7 copy.15
Async XLA Ops:
  74.1 1.7 %copy-start = (bf16[32,32,128]{2,1,0:T(8,128)(2,1)S(1)}, bf16[32,32,128]{2,1,0:T(8,128)(2,1)}, u32[]{:S(2)}) copy-start(bf16[32,32,128]{2,1,0:T(8,128)(2,1)} %get-tuple-element.5) | copy-start | bytes 786436

commit v4 on v3

v4 whole, which is shorter than its diff:
```python
import jax
import jax.numpy as jnp
from jax import lax
from jax.experimental import pallas as pl
from jax.experimental.pallas import tpu as pltpu
from jax.sharding import PartitionSpec as P

epsilon = 1e-05
MESH = pl.DeviceIdType.MESH
F32 = jnp.float32
BF16 = jnp.bfloat16

U = 8
G = 4
V = 4
TILE = 32
LANES = 128
CHAN = 128
WIDE = 256


def dot(a, b):
    return lax.dot_general(a, b, (((1,), (0,)), ((), ())), preferred_element_type=F32)


def dot_nt(a, b):
    return lax.dot_general(a, b, (((1,), (1,)), ((), ())), preferred_element_type=F32)


def dot_tn(a, b):
    return lax.dot_general(a, b, (((0,), (0,)), ((), ())), preferred_element_type=F32)


def swap_groups(parts):
    lane = lax.broadcasted_iota(jnp.int32, parts[0].shape, 1)
    low = lane < 64
    even = (lane // 32) % 2 == 0
    half = [[None, None], [None, None]]
    for bit in range(2):
        a, b = parts[bit], parts[2 + bit]
        half[0][bit] = jnp.where(low, a, pltpu.roll(b, 64, 1))
        half[1][bit] = jnp.where(low, pltpu.roll(a, 64, 1), b)
    out = []
    for bit in range(2):
        a, b = half[bit]
        out.append(jnp.where(even, a, pltpu.roll(b, 32, 1)))
        out.append(jnp.where(even, pltpu.roll(a, 96, 1), b))
    return out


def normalize(values, gain, bias):
    average = jnp.mean(values, axis=0, keepdims=True)
    centred = values - average
    inverse = lax.rsqrt(jnp.mean(centred * centred, axis=0, keepdims=True) + epsilon)
    scaled = centred * inverse
    return scaled * gain + bias, scaled, inverse


def norm_back(grad, gain, scaled, inverse):
    s = grad * gain
    first = jnp.mean(s, axis=0, keepdims=True)
    second = jnp.mean(s * scaled, axis=0, keepdims=True)
    return (s - first - scaled * second) * inverse


def tile_of(ref, v):
    rows = [ref[g * U + 2 * v + e] for e in range(2) for g in range(G)]
    return jnp.concatenate(rows, axis=0).astype(F32).T


def store_tile(ref, v, values):
    whole = values.T.astype(BF16)
    for e in range(2):
        for g in range(G):
            at = (e * G + g) * TILE
            ref[g * U + 2 * v + e] = whole[at : at + TILE, :]


def kernel(
    pair_hbm, mask_hbm, cot_hbm, w_in_hbm, w_out_hbm, w_gout_hbm,
    gain_in_hbm, bias_in_hbm, gain_out_hbm, bias_out_hbm,
    out_ref, grad_ref,
    pair_ref, mask_ref, cot_ref, w_in_ref, w_out_ref, w_gout_ref,
    gain_in_ref, bias_in_ref, gain_out_ref, bias_out_ref,
    w_side, w_side_t, w_out_t, w_gout_t, masks, normed_s, scaled_s, inv_s,
    factor_s, ogate_s, cot_s, oproj_s, ggate_s,
    stage, tile_out, tile_in, owner_out, owner_in, left_m, right_m, grad_m, swap_s, swap_r,
    tile_send, tile_recv, owner_send, owner_recv, csend, crecv, local_sem, ready_sem,
):
    arrays = [
        (pair_hbm, pair_ref), (mask_hbm, mask_ref), (w_in_hbm, w_in_ref), (w_out_hbm, w_out_ref),
        (w_gout_hbm, w_gout_ref), (gain_in_hbm, gain_in_ref), (bias_in_hbm, bias_in_ref),
        (gain_out_hbm, gain_out_ref), (bias_out_hbm, bias_out_ref), (cot_hbm, cot_ref),
    ]
    loads = [
        pltpu.make_async_copy(src, dst, local_sem.at[i]) for i, (src, dst) in enumerate(arrays)
    ]
    for load in loads:
        load.start()

    row = lax.axis_index("row")
    col = lax.axis_index("col")
    z = row % 8
    x_hi = row // 8
    core = col % 2
    q = col // 2
    side = row % 2
    block = row // 2
    chan = row * 8 + q
    partner = (row, col + 1 - 2 * core)

    barrier = pltpu.get_barrier_semaphore()

    def plane_peer(d):
        peer = (x_hi * 8 + q + d) % 16
        return ((peer // 8) * 8 + z, (peer % 8) * 2 + core)

    @pl.loop(1, 16)
    def _(d):
        peer = (z * 2 + core + d) % 16
        where = (x_hi * 8 + peer // 2, q * 2 + peer % 2)
        pl.semaphore_signal(barrier, inc=1, device_id=where, device_id_type=MESH)

    @pl.loop(1, 16)
    def _(d):
        pl.semaphore_signal(barrier, inc=1, device_id=plane_peer(d), device_id_type=MESH)

    def to_owner(t, c):
        return pltpu.make_async_remote_copy(
            src_ref=tile_out.at[t, c],
            dst_ref=owner_in.at[t, block, col],
            send_sem=tile_send.at[t],
            recv_sem=owner_recv.at[t],
            device_id=(c // 8, (c % 8) * 2 + side),
            device_id_type=MESH,
        )

    def send_owners(t):
        @pl.when(side == core)
        def _():
            pltpu.make_async_copy(
                tile_out.at[t, chan], owner_in.at[t, block, col], owner_recv.at[t]
            ).start()

        @pl.when(side != core)
        def _():
            to_owner(t, chan).start()

        @pl.loop(1, 128)
        def _(d):
            to_owner(t, (chan + d) % 128).start()

    def to_tile(t, to_block, to_col):
        return pltpu.make_async_remote_copy(
            src_ref=owner_out.at[t, to_block, to_col],
            dst_ref=tile_in.at[t, chan],
            send_sem=owner_send.at[t],
            recv_sem=tile_recv.at[t],
            device_id=(to_block * 2 + core, to_col),
            device_id_type=MESH,
        )

    def send_tiles(t, half):
        own = jnp.logical_and(side == core, core == half)

        @pl.when(own)
        def _():
            pltpu.make_async_copy(
                owner_out.at[t, block, col], tile_in.at[t, chan], tile_recv.at[t]
            ).start()

        @pl.when(jnp.logical_not(own))
        def _():
            to_tile(t, block, q * 2 + half).start()

        @pl.loop(1, 64)
        def _(d):
            to = (block * 8 + q + d) % 64
            to_tile(t, to // 8, (to % 8) * 2 + half).start()

    def owner_receive(t):
        pltpu.make_async_copy(owner_out.at[t], owner_in.at[t], owner_recv.at[t]).wait()

    def tile_receive(t):
        pltpu.make_async_copy(tile_out.at[t], tile_in.at[t], tile_recv.at[t]).wait()

    def all_sent():
        for t in range(3):
            for ref, sem in ((tile_out.at[t], tile_send.at[t]), (owner_out.at[t], owner_send.at[t])):

                @pl.when(side != core)
                def _():
                    pltpu.make_async_copy(ref, ref, sem).wait()

            @pl.when(side == core)
            def _():
                ref = tile_out.at[t, pl.ds(0, 127)]
                pltpu.make_async_copy(ref, ref, tile_send.at[t]).wait()
                for part in (owner_out.at[t, pl.ds(0, 7)], owner_out.at[t, 7, pl.ds(0, 15)]):
                    pltpu.make_async_copy(part, part, owner_send.at[t]).wait()

    def gather(t):
        for at in range(4):
            parts = [
                owner_in[t, :, ((at % 2) * 4 + p) * 2 + at // 2].astype(F32).reshape(64, LANES)
                for p in range(4)
            ]
            moved = [m.reshape(8, 1, U, LANES) for m in swap_groups(parts)]
            yield at, jnp.concatenate(moved, axis=1).reshape(WIDE, LANES).astype(BF16)

    def scatter(t, half, values):
        for at in range(2):
            tiles = values[:, at * LANES : at * LANES + LANES].reshape(8, G, U, LANES)
            parts = [tiles[:, g].reshape(64, LANES) for g in range(G)]
            for p, moved in enumerate(swap_groups(parts)):
                owner_out[t, :, (at * 4 + p) * 2 + half] = moved.reshape(8, U, LANES).astype(BF16)

    def to_partner(i, src, dst):
        return pltpu.make_async_remote_copy(
            src_ref=src,
            dst_ref=dst,
            send_sem=csend.at[i],
            recv_sem=crecv.at[i],
            device_id=partner,
            device_id_type=MESH,
        )

    def halves(x):
        return [x[:, 0:LANES], x[:, LANES : 2 * LANES]]

    def strided(v, e):
        return pl.ds(2 * v + e, CHAN, stride=U)

    def put(t, v, values):
        for e, value in enumerate(halves(values)):
            stage[t, strided(v, e), :] = value

    def get(t, v):
        return jnp.concatenate([stage[t, strided(v, e), :] for e in range(2)], axis=1)

    def pack(t):
        tile_out[t] = stage[t].reshape(CHAN, U, LANES).astype(BF16)

    def unpack(t):
        stage[3 + t] = tile_in[t].astype(F32).reshape(CHAN * U, LANES)

    for load in loads[1:9]:
        load.wait()
    for t in range(2):
        for part in range(2):
            base = (2 * part + t) * CHAN
            piece = w_in_ref[:, base : base + CHAN]
            w_side[t, :, part * CHAN : part * CHAN + CHAN] = piece
            w_side_t[t, part * CHAN : part * CHAN + CHAN, :] = piece.astype(F32).T.astype(BF16)
    w_out_t[...] = w_out_ref[...].astype(F32).T.astype(BF16)
    w_gout_t[...] = w_gout_ref[...].astype(F32).T.astype(BF16)

    def column(ref):
        return jnp.broadcast_to(ref[...].reshape(1, CHAN), (8, CHAN)).T[:, 0:1]

    gain_in = column(gain_in_ref)
    bias_in = column(bias_in_ref)
    gain_out = column(gain_out_ref)
    bias_out = column(bias_out_ref)

    valid = jnp.broadcast_to(mask_ref[...].reshape(1, 512), (8, 512)).astype(F32).astype(BF16)
    number = lax.broadcasted_iota(jnp.int32, (512, WIDE), 0)
    place = lax.broadcasted_iota(jnp.int32, (512, WIDE), 1)
    col_pick = (number == col * TILE + place % 32).astype(F32).astype(BF16)
    col_valid = dot(valid, col_pick)
    for v in range(V):
        first = row * TILE + ((place // 32) % G) * U + place // LANES + 2 * v
        row_pick = (number == first).astype(F32).astype(BF16)
        masks[v] = (dot(valid, row_pick) * col_valid)[0:1, :]

    def branch(t, v, normed):
        mixed = dot(w_side_t[t], normed)
        projected = mixed[0:CHAN, :]
        gates = jax.nn.sigmoid(mixed[CHAN : 2 * CHAN, :])
        mask = masks[v]
        value = gates * projected * mask
        factor_s[t, v, 0:CHAN, :] = gates * mask
        factor_s[t, v, CHAN : 2 * CHAN, :] = value * (1.0 - gates)
        put(t, v, value)

    loads[0].wait()

    @pl.loop(0, V)
    def _(v):
        normed, scaled, inverse = normalize(tile_of(pair_ref, v), gain_in, bias_in)
        normed = normed.astype(BF16)
        normed_s[v] = normed
        scaled_s[v] = scaled
        inv_s[v] = inverse
        branch(1, v, normed)

    pack(1)
    pl.semaphore_wait(barrier, 15 + 15)

    @pl.loop(1, 16)
    def _(d):
        pl.semaphore_signal(ready_sem, inc=1, device_id=plane_peer(d), device_id_type=MESH)

    @pl.loop(0, V)
    def _(v):
        branch(0, v, normed_s[v])

    pack(0)
    pl.semaphore_wait(ready_sem, 15)
    send_owners(1)
    send_owners(0)

    loads[9].wait()

    @pl.loop(0, V)
    def _(v):
        ogate_s[v] = jax.nn.sigmoid(dot(w_gout_t[...], normed_s[v]))
        cot_s[v] = tile_of(cot_ref, v)

    owner_receive(1)
    for at, value in gather(1):
        right_m[core, :, at * LANES : at * LANES + LANES] = value
    right_copy = to_partner(0, right_m.at[core], right_m.at[core])
    right_copy.start()
    owner_receive(0)
    for at, value in gather(0):
        left_m[:, at * LANES : at * LANES + LANES] = value
    right_copy.wait_recv()
    for half in range(2):
        scatter(0, half, dot_nt(left_m[...], right_m[half]))
        send_tiles(0, half)
    tile_receive(0)

    unpack(0)

    @pl.loop(0, V)
    def _(v):
        out_norm, scaled, inverse = normalize(get(3, v), gain_out, bias_out)
        outer_proj = dot(w_out_t[...], out_norm.astype(BF16))
        gated = cot_s[v] * ogate_s[v]
        grad_outnorm = dot(w_out_ref[...], gated.astype(BF16))
        oproj_s[v] = outer_proj
        put(2, v, norm_back(grad_outnorm, gain_out, scaled, inverse))

    pack(2)
    send_owners(2)

    @pl.loop(0, V)
    def _(v):
        outer_proj = oproj_s[v]
        outer_gate = ogate_s[v]
        store_tile(out_ref, v, outer_gate * outer_proj)
        grad_gate = (cot_s[v] * outer_proj * outer_gate * (1.0 - outer_gate)).astype(BF16)
        ggate_s[v] = dot(w_gout_ref[...], grad_gate)

    owner_receive(2)
    for at, value in gather(2):
        grad_m[at // 2, :, (at % 2) * LANES : (at % 2) * LANES + LANES] = value

    def part(half):
        return slice(half * WIDE, half * WIDE + WIDE)

    def left_part(half):
        grad = dot(grad_m[0], right_m[0, :, part(half)])
        scatter(1, half, grad + dot(grad_m[1], right_m[1, :, part(half)]))
        send_tiles(1, half)

    left_part(0)
    swap_s[...] = dot_tn(grad_m[1 - core], left_m[...]).astype(BF16)
    grad_copy = to_partner(1, swap_s, swap_r)
    grad_copy.start()
    left_part(1)
    grad_copy.wait_recv()
    for half in range(2):
        grad = dot_tn(grad_m[core], left_m[:, part(half)])
        scatter(2, half, grad + swap_r[:, part(half)].astype(F32))
        send_tiles(2, half)

    def mixed(t, v):
        grad = get(4 + t, v)
        return jnp.concatenate([grad, grad], axis=0) * factor_s[t, v]

    tile_receive(1)
    unpack(1)

    @pl.loop(0, V)
    def _(v):
        ggate_s[v] += dot(w_side[0], mixed(0, v).astype(BF16))

    tile_receive(2)
    unpack(2)

    @pl.loop(0, V)
    def _(v):
        grad_normed = ggate_s[v] + dot(w_side[1], mixed(1, v).astype(BF16))
        store_tile(grad_ref, v, norm_back(grad_normed, gain_in, scaled_s[v], inv_s[v]))

    all_sent()
    right_copy.wait_send()
    grad_copy.wait_send()


def per_device(
    pair, residue_mask, cotangent, w_in, w_out, w_gout, gain_in, bias_in, gain_out, bias_out
):
    hbm = pl.BlockSpec(memory_space=pl.ANY)
    vmem = pl.BlockSpec(memory_space=pltpu.VMEM)
    shape = jax.ShapeDtypeStruct(pair.shape, BF16)
    args = (
        pair, residue_mask, cotangent, w_in, w_out, w_gout, gain_in, bias_in, gain_out, bias_out
    )
    return pl.pallas_call(
        kernel,
        out_shape=(shape, shape),
        in_specs=[hbm] * 10,
        out_specs=(vmem, vmem),
        scratch_shapes=[pltpu.VMEM(a.shape, a.dtype) for a in args]
        + [
            pltpu.VMEM((2, CHAN, 2 * CHAN), BF16),
            pltpu.VMEM((2, 2 * CHAN, CHAN), BF16),
            pltpu.VMEM((CHAN, CHAN), BF16),
            pltpu.VMEM((CHAN, CHAN), BF16),
            pltpu.VMEM((V, 1, WIDE), F32),
            pltpu.VMEM((V, CHAN, WIDE), BF16),
            pltpu.VMEM((V, CHAN, WIDE), F32),
            pltpu.VMEM((V, 1, WIDE), F32),
            pltpu.VMEM((2, V, 2 * CHAN, WIDE), F32),
            pltpu.VMEM((V, CHAN, WIDE), F32),
            pltpu.VMEM((V, CHAN, WIDE), F32),
            pltpu.VMEM((V, CHAN, WIDE), F32),
            pltpu.VMEM((V, CHAN, WIDE), F32),
            pltpu.VMEM((6, CHAN * U, LANES), F32),
            pltpu.VMEM((3, CHAN, U, LANES), BF16),
            pltpu.VMEM((3, CHAN, U, LANES), BF16),
            pltpu.VMEM((3, 8, 16, U, LANES), BF16),
            pltpu.VMEM((3, 8, 16, U, LANES), BF16),
            pltpu.VMEM((WIDE, 2 * WIDE), BF16),
            pltpu.VMEM((2, WIDE, 2 * WIDE), BF16),
            pltpu.VMEM((2, WIDE, WIDE), BF16),
            pltpu.VMEM((WIDE, 2 * WIDE), BF16),
            pltpu.VMEM((WIDE, 2 * WIDE), BF16),
            pltpu.SemaphoreType.DMA((3,)),
            pltpu.SemaphoreType.DMA((3,)),
            pltpu.SemaphoreType.DMA((3,)),
            pltpu.SemaphoreType.DMA((3,)),
            pltpu.SemaphoreType.DMA((2,)),
            pltpu.SemaphoreType.DMA((2,)),
            pltpu.SemaphoreType.DMA((10,)),
            pltpu.SemaphoreType.REGULAR,
        ],
        compiler_params=pltpu.CompilerParams(
            collective_id=0, has_side_effects=True, vmem_limit_bytes=60 * 1024 * 1024
        ),
    )(*args)


def solution(mesh):
    tile = P("row", "col", None)
    return jax.shard_map(
        per_device,
        mesh=mesh,
        in_specs=(tile, P(), tile, P(), P(), P(), P(), P(), P(), P()),
        out_specs=(tile, tile),
        check_vma=False,
    )
```

time: 76.7 us -> 74.6 us (0.973)
  Pallas kernels: 73.5 us -> 71.4 us
    pallas_call x1, Pallas kernels: 73.5 us -> 71.4 us  [per_device(): pl.pallas_call(kernel, out_shape=(shape, shape), in_specs=[hbm] * 10, out...]
where the time goes in v4:
time: 74.6 us; the launch traced here: 74.5 us
  Pallas kernels  71.4 us (96%)
  local copies, waits for them, and re-layouts  2.42 us (3%)
    pallas_call x1, Pallas kernels, per_device(): pl.pallas_call(kernel, out_shape=(shape, shape), in_specs=[hbm] * 10, out...  71.4 us
    unnamed x4, local copies, waits for them, and re-layouts  2.42 us

profile of v4, /device:TPU:1, one launch (start us, length us, event | category | flops | bytes accessed | tf_op | source)
XLA Modules:
  0.0 74.5 jit_solution(1007592852948828578)
XLA Ops:
  0.6 71.4 %shard_map.113 = (bf16[32,32,128]{2,1,0:T(8,128)(2,1)}, bf16[32,32,128]{2,1,0:T(8,128)(2,1)}) custom-call(bf16[32,32,128]{2,1,0:T(8,128)(2,1)} %pair_hbm.1, s32[512]{0:T(512)} %mask_hbm.1, bf16[32,32,128]{2,1,0:T(8,128)(2,1)} %cot_hbm.1, bf16[128,512]{1,0:T(8,128)(2,1)} %w_in_hbm.1, bf16[128,128]{1,0:T(8,128)(2,1)} %w_out_hbm.1, ...), custom_call_target="tpu_custom_call" | custom-call | tf_op jit(solution)/shard_map/pallas_call | solution.py:412
  72.0 0.0 copy-start
  72.1 1.7 %copy.14 = bf16[32,32,128]{2,1,0:T(8,128)(2,1)} copy(bf16[32,32,128]{2,1,0:T(8,128)(2,1)} %get-tuple-element.4) | data formatting | bytes 524288
  73.8 0.0 copy-done
  73.8 0.7 copy.15
Async XLA Ops:
  72.0 1.7 %copy-start = (bf16[32,32,128]{2,1,0:T(8,128)(2,1)S(1)}, bf16[32,32,128]{2,1,0:T(8,128)(2,1)}, u32[]{:S(2)}) copy-start(bf16[32,32,128]{2,1,0:T(8,128)(2,1)} %get-tuple-element.5) | copy-start | bytes 786436

commit v5 on v4

--- a/solution.py
+++ b/solution.py
@@ -285,7 +285,7 @@
 
     loads[0].wait()
 
-    @pl.loop(0, V)
+    @pl.loop(0, V, unroll=True)
     def _(v):
         normed, scaled, inverse = normalize(tile_of(pair_ref, v), gain_in, bias_in)
         normed = normed.astype(BF16)
@@ -301,7 +301,7 @@
     def _(d):
         pl.semaphore_signal(ready_sem, inc=1, device_id=plane_peer(d), device_id_type=MESH)
 
-    @pl.loop(0, V)
+    @pl.loop(0, V, unroll=True)
     def _(v):
         branch(0, v, normed_s[v])
 
@@ -312,7 +312,7 @@
 
     loads[9].wait()
 
-    @pl.loop(0, V)
+    @pl.loop(0, V, unroll=True)
     def _(v):
         ogate_s[v] = jax.nn.sigmoid(dot(w_gout_t[...], normed_s[v]))
         cot_s[v] = tile_of(cot_ref, v)
@@ -333,7 +333,7 @@
 
     unpack(0)
 
-    @pl.loop(0, V)
+    @pl.loop(0, V, unroll=True)
     def _(v):
         out_norm, scaled, inverse = normalize(get(3, v), gain_out, bias_out)
         outer_proj = dot(w_out_t[...], out_norm.astype(BF16))
@@ -345,7 +345,7 @@
     pack(2)
     send_owners(2)
 
-    @pl.loop(0, V)
+    @pl.loop(0, V, unroll=True)
     def _(v):
         outer_proj = oproj_s[v]
         outer_gate = ogate_s[v]
@@ -383,14 +383,14 @@
     tile_receive(1)
     unpack(1)
 
-    @pl.loop(0, V)
+    @pl.loop(0, V, unroll=True)
     def _(v):
         ggate_s[v] += dot(w_side[0], mixed(0, v).astype(BF16))
 
     tile_receive(2)
     unpack(2)
 
-    @pl.loop(0, V)
+    @pl.loop(0, V, unroll=True)
     def _(v):
         grad_normed = ggate_s[v] + dot(w_side[1], mixed(1, v).astype(BF16))
         store_tile(grad_ref, v, norm_back(grad_normed, gain_in, scaled_s[v], inv_s[v]))
@@ -449,9 +449,9 @@
             pltpu.SemaphoreType.REGULAR,
         ],
         compiler_params=pltpu.CompilerParams(
-            collective_id=0, has_side_effects=True, vmem_limit_bytes=60 * 1024 * 1024
+            collective_id=0, has_side_effects=True, vmem_limit_bytes=48 * 1024 * 1024
         ),
-    )(*args)
+    )(*[pltpu.with_memory_space_constraint(a, pltpu.HBM) for a in args])
 
 
 def solution(mesh):

time: 74.6 us -> 71.6 us (0.960)
  Pallas kernels: 71.4 us -> 69.5 us
  local copies, waits for them, and re-layouts: 2.42 us -> 1.41 us
    pallas_call x1, Pallas kernels: 71.4 us -> 69.5 us  [per_device(): pl.pallas_call(kernel, out_shape=(shape, shape), in_specs=[hbm] * 10, out...]
    unnamed x4 -> x2, local copies, waits for them, and re-layouts: 2.42 us -> 1.41 us
where the time goes in v5:
time: 71.6 us; the launch traced here: 71.5 us
  Pallas kernels  69.5 us (97%)
  local copies, waits for them, and re-layouts  1.41 us (2%)
    pallas_call x1, Pallas kernels, per_device(): pl.pallas_call(kernel, out_shape=(shape, shape), in_specs=[hbm] * 10, out...  69.5 us

profile of v5, /device:TPU:1, one launch (start us, length us, event | category | flops | bytes accessed | tf_op | source)
XLA Modules:
  0.0 71.5 jit_solution(7467844004717003377)
XLA Ops:
  0.6 69.5 %shard_map.113 = (bf16[32,32,128]{2,1,0:T(8,128)(2,1)S(1)}, bf16[32,32,128]{2,1,0:T(8,128)(2,1)S(1)}) custom-call(bf16[32,32,128]{2,1,0:T(8,128)(2,1)} %pair_hbm.1, s32[512]{0:T(512)} %mask_hbm.1, bf16[32,32,128]{2,1,0:T(8,128)(2,1)} %cot_hbm.1, bf16[128,512]{1,0:T(8,128)(2,1)} %w_in_hbm.1, bf16[128,128]{1,0:T(8,128)(2,1)} %w_out_hbm.1, ...), custom_call_target="tpu_custom_call" | custom-call | tf_op jit(solution)/shard_map/pallas_call | solution.py:412
  70.1 0.7 copy.14
  70.8 0.7 copy.15

commit v6 on v5

--- a/solution.py
+++ b/solution.py
@@ -84,7 +84,7 @@
     gain_in_ref, bias_in_ref, gain_out_ref, bias_out_ref,
     w_side, w_side_t, w_out_t, w_gout_t, masks, normed_s, scaled_s, inv_s,
     factor_s, ogate_s, cot_s, oproj_s, ggate_s,
-    stage, tile_out, tile_in, owner_out, owner_in, left_m, right_m, grad_m, swap_s, swap_r,
+    stage, tile_out, tile_in, owner_out, owner_in, left_m, right_m, grad_m, swap_s, swap_r, left_s,
     tile_send, tile_recv, owner_send, owner_recv, csend, crecv, local_sem, ready_sem,
 ):
     arrays = [
@@ -130,7 +130,7 @@
             src_ref=tile_out.at[t, c],
             dst_ref=owner_in.at[t, block, col],
             send_sem=tile_send.at[t],
-            recv_sem=owner_recv.at[t],
+            recv_sem=owner_recv.at[t, col // 8],
             device_id=(c // 8, (c % 8) * 2 + side),
             device_id_type=MESH,
         )
@@ -139,7 +139,7 @@
         @pl.when(side == core)
         def _():
             pltpu.make_async_copy(
-                tile_out.at[t, chan], owner_in.at[t, block, col], owner_recv.at[t]
+                tile_out.at[t, chan], owner_in.at[t, block, col], owner_recv.at[t, col // 8]
             ).start()
 
         @pl.when(side != core)
@@ -160,9 +160,7 @@
             device_id_type=MESH,
         )
 
-    def send_tiles(t, half):
-        own = jnp.logical_and(side == core, core == half)
-
+    def send_some(t, own, to_block, to_col, where, count):
         @pl.when(own)
         def _():
             pltpu.make_async_copy(
@@ -171,15 +169,34 @@
 
         @pl.when(jnp.logical_not(own))
         def _():
-            to_tile(t, block, q * 2 + half).start()
-
-        @pl.loop(1, 64)
+            to_tile(t, to_block, to_col).start()
+
+        @pl.loop(1, count)
         def _(d):
-            to = (block * 8 + q + d) % 64
-            to_tile(t, to // 8, (to % 8) * 2 + half).start()
-
-    def owner_receive(t):
-        pltpu.make_async_copy(owner_out.at[t], owner_in.at[t], owner_recv.at[t]).wait()
+            to_tile(t, *where(d)).start()
+
+    def send_part(t, at):
+        p, h = at // 2, at % 2
+
+        def where(d):
+            to = (block * 4 + q % 4 + d) % 32
+            return to // 4, (h * 4 + to % 4) * 2 + p
+
+        own = jnp.logical_and(side == core, jnp.logical_and(q // 4 == h, core == p))
+        send_some(t, own, block, (h * 4 + q % 4) * 2 + p, where, 32)
+
+    def send_blocks(t, half):
+        def where(d):
+            to = ((block % 4) * 16 + col + d) % 64
+            return half * 4 + to // 16, to % 16
+
+        own = jnp.logical_and(side == core, block // 4 == half)
+        send_some(t, own, half * 4 + block % 4, col, where, 64)
+
+    def owner_receive(t, parts=(0, 1)):
+        for h in parts:
+            ref = owner_in.at[t, :, pl.ds(h * 8, 8)]
+            pltpu.make_async_copy(ref, ref, owner_recv.at[t, h]).wait()
 
     def tile_receive(t):
         pltpu.make_async_copy(tile_out.at[t], tile_in.at[t], tile_recv.at[t]).wait()
@@ -199,21 +216,24 @@
                 for part in (owner_out.at[t, pl.ds(0, 7)], owner_out.at[t, 7, pl.ds(0, 15)]):
                     pltpu.make_async_copy(part, part, owner_send.at[t]).wait()
 
-    def gather(t):
-        for at in range(4):
-            parts = [
-                owner_in[t, :, ((at % 2) * 4 + p) * 2 + at // 2].astype(F32).reshape(64, LANES)
-                for p in range(4)
-            ]
-            moved = [m.reshape(8, 1, U, LANES) for m in swap_groups(parts)]
-            yield at, jnp.concatenate(moved, axis=1).reshape(WIDE, LANES).astype(BF16)
-
-    def scatter(t, half, values):
-        for at in range(2):
-            tiles = values[:, at * LANES : at * LANES + LANES].reshape(8, G, U, LANES)
-            parts = [tiles[:, g].reshape(64, LANES) for g in range(G)]
-            for p, moved in enumerate(swap_groups(parts)):
-                owner_out[t, :, (at * 4 + p) * 2 + half] = moved.reshape(8, U, LANES).astype(BF16)
+    def gather(t, at):
+        parts = [
+            owner_in[t, :, ((at % 2) * 4 + p) * 2 + at // 2].astype(F32).reshape(64, LANES)
+            for p in range(4)
+        ]
+        moved = [m.reshape(8, 1, U, LANES) for m in swap_groups(parts)]
+        return jnp.concatenate(moved, axis=1).reshape(WIDE, LANES).astype(BF16)
+
+    def scatter(t, at, values, blocks=slice(0, 8)):
+        count = values.shape[0] // TILE
+        tiles = values.reshape(count, G, U, LANES)
+        parts = [tiles[:, g].reshape(count * U, LANES) for g in range(G)]
+        for p, moved in enumerate(swap_groups(parts)):
+            to = ((at % 2) * 4 + p) * 2 + at // 2
+            owner_out[t, blocks, to] = moved.reshape(count, U, LANES).astype(BF16)
+
+    def lanes(at):
+        return slice(at * LANES, at * LANES + LANES)
 
     def to_partner(i, src, dst):
         return pltpu.make_async_remote_copy(
@@ -318,17 +338,24 @@
         cot_s[v] = tile_of(cot_ref, v)
 
     owner_receive(1)
-    for at, value in gather(1):
-        right_m[core, :, at * LANES : at * LANES + LANES] = value
+    for at in range(4):
+        value = gather(1, at)
+        for h in range(2):
+            right_m[core, h, :, lanes(at)] = value[h * LANES : h * LANES + LANES, :]
     right_copy = to_partner(0, right_m.at[core], right_m.at[core])
     right_copy.start()
     owner_receive(0)
-    for at, value in gather(0):
-        left_m[:, at * LANES : at * LANES + LANES] = value
+    for at in range(4):
+        left_m[:, lanes(at)] = gather(0, at)
     right_copy.wait_recv()
-    for half in range(2):
-        scatter(0, half, dot_nt(left_m[...], right_m[half]))
-        send_tiles(0, half)
+
+    def right_rows(h):
+        return jnp.concatenate([right_m[0, h], right_m[1, h]], axis=0)
+
+    for h in range(2):
+        for p in range(2):
+            scatter(0, 2 * p + h, dot_nt(left_m[...], right_m[p, h]))
+            send_part(0, 2 * p + h)
     tile_receive(0)
 
     unpack(0)
@@ -353,28 +380,39 @@
         grad_gate = (cot_s[v] * outer_proj * outer_gate * (1.0 - outer_gate)).astype(BF16)
         ggate_s[v] = dot(w_gout_ref[...], grad_gate)
 
-    owner_receive(2)
-    for at, value in gather(2):
-        grad_m[at // 2, :, (at % 2) * LANES : (at % 2) * LANES + LANES] = value
-
-    def part(half):
-        return slice(half * WIDE, half * WIDE + WIDE)
-
-    def left_part(half):
-        grad = dot(grad_m[0], right_m[0, :, part(half)])
-        scatter(1, half, grad + dot(grad_m[1], right_m[1, :, part(half)]))
-        send_tiles(1, half)
-
-    left_part(0)
-    swap_s[...] = dot_tn(grad_m[1 - core], left_m[...]).astype(BF16)
-    grad_copy = to_partner(1, swap_s, swap_r)
-    grad_copy.start()
-    left_part(1)
-    grad_copy.wait_recv()
-    for half in range(2):
-        grad = dot_tn(grad_m[core], left_m[:, part(half)])
-        scatter(2, half, grad + swap_r[:, part(half)].astype(F32))
-        send_tiles(2, half)
+    def grad_rows(h):
+        return jnp.concatenate([grad_m[h, 0], grad_m[h, 1]], axis=1)
+
+    grad_copies = [to_partner(1 + h, swap_s.at[h], swap_r.at[h]) for h in range(2)]
+
+    def swap_right(h):
+        swap_s[h] = dot_tn(grad_m[h, 1 - core], left_m[...]).astype(BF16)
+        grad_copies[h].start()
+
+    def send_right(h):
+        grad = dot_tn(grad_m[h, core], left_m[...])
+        grad_copies[h].wait_recv()
+        grad = grad + swap_r[h].astype(F32)
+        for at in range(4):
+            scatter(2, at, grad[:, lanes(at)], slice(4 * h, 4 * h + 4))
+        send_blocks(2, h)
+
+    owner_receive(2, (0,))
+    for p in range(2):
+        grad_m[0, p] = gather(2, 2 * p)
+    swap_right(0)
+    left_s[...] = dot(grad_rows(0), right_rows(0))
+    send_right(0)
+    owner_receive(2, (1,))
+    for p in range(2):
+        grad_m[1, p] = gather(2, 2 * p + 1)
+    for at in range(4):
+        grad = dot(grad_rows(1), right_rows(1)[:, lanes(at)])
+        scatter(1, at, left_s[:, lanes(at)] + grad)
+        send_part(1, at)
+        if at == 0:
+            swap_right(1)
+    send_right(1)
 
     def mixed(t, v):
         grad = get(4 + t, v)
@@ -396,8 +434,8 @@
         store_tile(grad_ref, v, norm_back(grad_normed, gain_in, scaled_s[v], inv_s[v]))
 
     all_sent()
-    right_copy.wait_send()
-    grad_copy.wait_send()
+    for copy in [right_copy] + grad_copies:
+        copy.wait_send()
 
 
 def per_device(
@@ -435,16 +473,17 @@
             pltpu.VMEM((3, 8, 16, U, LANES), BF16),
             pltpu.VMEM((3, 8, 16, U, LANES), BF16),
             pltpu.VMEM((WIDE, 2 * WIDE), BF16),
-            pltpu.VMEM((2, WIDE, 2 * WIDE), BF16),
-            pltpu.VMEM((2, WIDE, WIDE), BF16),
-            pltpu.VMEM((WIDE, 2 * WIDE), BF16),
-            pltpu.VMEM((WIDE, 2 * WIDE), BF16),
+            pltpu.VMEM((2, 2, LANES, 2 * WIDE), BF16),
+            pltpu.VMEM((2, 2, WIDE, LANES), BF16),
+            pltpu.VMEM((2, LANES, 2 * WIDE), BF16),
+            pltpu.VMEM((2, LANES, 2 * WIDE), BF16),
+            pltpu.VMEM((WIDE, 2 * WIDE), F32),
             pltpu.SemaphoreType.DMA((3,)),
             pltpu.SemaphoreType.DMA((3,)),
             pltpu.SemaphoreType.DMA((3,)),
+            pltpu.SemaphoreType.DMA((3, 2)),
             pltpu.SemaphoreType.DMA((3,)),
-            pltpu.SemaphoreType.DMA((2,)),
-            pltpu.SemaphoreType.DMA((2,)),
+            pltpu.SemaphoreType.DMA((3,)),
             pltpu.SemaphoreType.DMA((10,)),
             pltpu.SemaphoreType.REGULAR,
         ],

time: 71.6 us -> 70.1 us (0.979)
  the two profiles are of different devices: /device:TPU:1 before, /device:TPU:7 now
where the time goes in v6:
time: 70.1 us; the launch traced here: 70 us
  Pallas kernels  67.9 us (97%)
  local copies, waits for them, and re-layouts  1.41 us (2%)
    pallas_call x1, Pallas kernels, per_device(): pl.pallas_call(kernel, out_shape=(shape, shape), in_specs=[hbm] * 10, out...  67.9 us
    unnamed x2, local copies, waits for them, and re-layouts  1.41 us

profile of v6, /device:TPU:7, one launch (start us, length us, event | category | flops | bytes accessed | tf_op | source)
XLA Modules:
  0.0 70.0 jit_solution(6519839922817474939)
XLA Ops:
  0.6 67.9 %shard_map.113 = (bf16[32,32,128]{2,1,0:T(8,128)(2,1)S(1)}, bf16[32,32,128]{2,1,0:T(8,128)(2,1)S(1)}) custom-call(bf16[32,32,128]{2,1,0:T(8,128)(2,1)} %pair_hbm.1, s32[512]{0:T(512)} %mask_hbm.1, bf16[32,32,128]{2,1,0:T(8,128)(2,1)} %cot_hbm.1, bf16[128,512]{1,0:T(8,128)(2,1)} %w_in_hbm.1, bf16[128,128]{1,0:T(8,128)(2,1)} %w_out_hbm.1, ...), custom_call_target="tpu_custom_call" | custom-call | tf_op jit(solution)/shard_map/pallas_call | solution.py:450
  68.6 0.7 %copy.14 = bf16[32,32,128]{2,1,0:T(8,128)(2,1)} copy(bf16[32,32,128]{2,1,0:T(8,128)(2,1)S(1)} %get-tuple-element.4) | data formatting | bytes 524288
  69.3 0.7 %copy.15 = bf16[32,32,128]{2,1,0:T(8,128)(2,1)} copy(bf16[32,32,128]{2,1,0:T(8,128)(2,1)S(1)} %get-tuple-element.5) | data formatting | bytes 524288

commit v7 on v6

--- a/solution.py
+++ b/solution.py
@@ -259,10 +259,10 @@
         return jnp.concatenate([stage[t, strided(v, e), :] for e in range(2)], axis=1)
 
     def pack(t):
-        tile_out[t] = stage[t].reshape(CHAN, U, LANES).astype(BF16)
+        tile_out[t] = stage[t, 0 : CHAN * U].reshape(CHAN, U, LANES).astype(BF16)
 
     def unpack(t):
-        stage[3 + t] = tile_in[t].astype(F32).reshape(CHAN * U, LANES)
+        stage[3 + t, 0 : CHAN * U] = tile_in[t].astype(F32).reshape(CHAN * U, LANES)
 
     for load in loads[1:9]:
         load.wait()
@@ -467,7 +467,7 @@
             pltpu.VMEM((V, CHAN, WIDE), F32),
             pltpu.VMEM((V, CHAN, WIDE), F32),
             pltpu.VMEM((V, CHAN, WIDE), F32),
-            pltpu.VMEM((6, CHAN * U, LANES), F32),
+            pltpu.VMEM((6, CHAN * U + U, LANES), F32),
             pltpu.VMEM((3, CHAN, U, LANES), BF16),
             pltpu.VMEM((3, CHAN, U, LANES), BF16),
             pltpu.VMEM((3, 8, 16, U, LANES), BF16),

time: 70.1 us -> 70.1 us (level)
  no operation moved by 1% of the time
where the time goes in v7:
time: 70.1 us; the launch traced here: 70 us
  Pallas kernels  68 us (97%)
  local copies, waits for them, and re-layouts  1.41 us (2%)
    pallas_call x1, Pallas kernels, per_device(): pl.pallas_call(kernel, out_shape=(shape, shape), in_specs=[hbm] * 10, out...  68 us
    unnamed x2, local copies, waits for them, and re-layouts  1.41 us

profile of v7, /device:TPU:7, one launch (start us, length us, event | category | flops | bytes accessed | tf_op | source)
XLA Modules:
  0.0 70.0 jit_solution(15926693029176163619)
XLA Ops:
  0.6 68.0 %shard_map.113 = (bf16[32,32,128]{2,1,0:T(8,128)(2,1)S(1)}, bf16[32,32,128]{2,1,0:T(8,128)(2,1)S(1)}) custom-call(bf16[32,32,128]{2,1,0:T(8,128)(2,1)} %pair_hbm.1, s32[512]{0:T(512)} %mask_hbm.1, bf16[32,32,128]{2,1,0:T(8,128)(2,1)} %cot_hbm.1, bf16[128,512]{1,0:T(8,128)(2,1)} %w_in_hbm.1, bf16[128,128]{1,0:T(8,128)(2,1)} %w_out_hbm.1, ...), custom_call_target="tpu_custom_call" | custom-call | tf_op jit(solution)/shard_map/pallas_call | solution.py:450
  68.6 0.7 %copy.14 = bf16[32,32,128]{2,1,0:T(8,128)(2,1)} copy(bf16[32,32,128]{2,1,0:T(8,128)(2,1)S(1)} %get-tuple-element.4) | data formatting | bytes 524288
  69.3 0.7 %copy.15 = bf16[32,32,128]{2,1,0:T(8,128)(2,1)} copy(bf16[32,32,128]{2,1,0:T(8,128)(2,1)S(1)} %get-tuple-element.5) | data formatting | bytes 524288

commit v8 on v7

--- a/solution.py
+++ b/solution.py
@@ -185,13 +185,16 @@
         own = jnp.logical_and(side == core, jnp.logical_and(q // 4 == h, core == p))
         send_some(t, own, block, (h * 4 + q % 4) * 2 + p, where, 32)
 
-    def send_blocks(t, half):
+    def send_blocks(t, half, at):
+        p, h = at // 2, at % 2
+
         def where(d):
-            to = ((block % 4) * 16 + col + d) % 64
-            return half * 4 + to // 16, to % 16
-
-        own = jnp.logical_and(side == core, block // 4 == half)
-        send_some(t, own, half * 4 + block % 4, col, where, 64)
+            to = ((block % 4) * 4 + q % 4 + d) % 16
+            return half * 4 + to // 4, (h * 4 + to % 4) * 2 + p
+
+        own = jnp.logical_and(block // 4 == half, jnp.logical_and(q // 4 == h, core == p))
+        own = jnp.logical_and(side == core, own)
+        send_some(t, own, half * 4 + block % 4, (h * 4 + q % 4) * 2 + p, where, 16)
 
     def owner_receive(t, parts=(0, 1)):
         for h in parts:
@@ -390,12 +393,13 @@
         grad_copies[h].start()
 
     def send_right(h):
-        grad = dot_tn(grad_m[h, core], left_m[...])
-        grad_copies[h].wait_recv()
-        grad = grad + swap_r[h].astype(F32)
         for at in range(4):
-            scatter(2, at, grad[:, lanes(at)], slice(4 * h, 4 * h + 4))
-        send_blocks(2, h)
+            grad = dot_tn(grad_m[h, core], left_m[:, lanes(at)])
+            if at == 0:
+                grad_copies[h].wait_recv()
+            grad = grad + swap_r[h, :, lanes(at)].astype(F32)
+            scatter(2, at, grad, slice(4 * h, 4 * h + 4))
+            send_blocks(2, h, at)
 
     owner_receive(2, (0,))
     for p in range(2):

time: 70.1 us -> 70.2 us (level)
  no operation moved by 1% of the time
where the time goes in v8:
time: 70.2 us; the launch traced here: 70.1 us
  Pallas kernels  68 us (97%)
  local copies, waits for them, and re-layouts  1.41 us (2%)
    pallas_call x1, Pallas kernels, per_device(): pl.pallas_call(kernel, out_shape=(shape, shape), in_specs=[hbm] * 10, out...  68 us
    unnamed x2, local copies, waits for them, and re-layouts  1.41 us

profile of v8, /device:TPU:7, one launch (start us, length us, event | category | flops | bytes accessed | tf_op | source)
XLA Modules:
  0.0 70.1 jit_solution(237118711581032544)
XLA Ops:
  0.6 68.0 %shard_map.113 = (bf16[32,32,128]{2,1,0:T(8,128)(2,1)S(1)}, bf16[32,32,128]{2,1,0:T(8,128)(2,1)S(1)}) custom-call(bf16[32,32,128]{2,1,0:T(8,128)(2,1)} %pair_hbm.1, s32[512]{0:T(512)} %mask_hbm.1, bf16[32,32,128]{2,1,0:T(8,128)(2,1)} %cot_hbm.1, bf16[128,512]{1,0:T(8,128)(2,1)} %w_in_hbm.1, bf16[128,128]{1,0:T(8,128)(2,1)} %w_out_hbm.1, ...), custom_call_target="tpu_custom_call" | custom-call | tf_op jit(solution)/shard_map/pallas_call | solution.py:454
  68.7 0.7 %copy.14 = bf16[32,32,128]{2,1,0:T(8,128)(2,1)} copy(bf16[32,32,128]{2,1,0:T(8,128)(2,1)S(1)} %get-tuple-element.4) | data formatting | bytes 524288
  69.4 0.7 %copy.15 = bf16[32,32,128]{2,1,0:T(8,128)(2,1)} copy(bf16[32,32,128]{2,1,0:T(8,128)(2,1)S(1)} %get-tuple-element.5) | data formatting | bytes 524288
